TPU v7x, 512 devices: a whole 4x4x16 slice. The times are simulated.
512 devices in a mesh: dp: 4 (over x), expert: 8 (over z_lo, core), tensor: 16 (over z_hi, y).
Axes of the slice: x: 4, y: 4, z: 16 (z_hi: 4, z_lo: 4; z = z_hi * 4 + z_lo), core: 2. Of those that a mesh axis runs over, the one named last changes fastest.
Arguments:
- pool: bfloat16 [512, 6144], P(('dp', 'expert'), 'tensor'), may hold values from -24 to 24
- prompt_ids: int32 [256, 24], replicated, may hold values from 0 to 511
- tenant: int32 [32], P(('dp', 'expert')), may hold values from 0 to 255
- lengths: int32 [32], P(('dp', 'expert')), may hold values from 1 to 24
- routes: int32 [768, 2], P(('dp', 'expert')), may hold values from 0 to 7, all different within a row; in each aligned block of 24 rows (0 to 23, 24 to 47, ...) at most 8 rows name the same one
- route_weight: float32 [768, 2], P(('dp', 'expert')), may hold values from 0.1 to 1
- cotangent: bfloat16 [768, 6144], P(('dp', 'expert'), 'tensor'), may hold values from -6 to 6
- norm_gain: bfloat16 [6144], replicated, may hold values from 0.3 to 3
- w_gate: bfloat16 [8, 6144, 8192], P('expert', None, ('dp', 'tensor')), may hold values from -0.078125 to 0.078125
- w_up: bfloat16 [8, 6144, 8192], P('expert', None, ('dp', 'tensor')), may hold values from -0.078125 to 0.078125
- w_down: bfloat16 [8, 8192, 6144], P('expert', ('dp', 'tensor')), may hold values from -0.0625 to 0.0625
Outputs:
- pool_grad: float32 [512, 6144], P(('dp', 'expert'), 'tensor')
Inputs may be any that keep to these rules, and one draw needn't show every extreme that they name: `routes`: in each aligned block of 24 rows (the rows of one sequence) no expert is named by more than 8 rows, a bound that some expert reaches in some or all blocks; the two experts of a row differ.
All inputs are finite; a program needn't handle non-finite values.
Results may differ from a plain program's by a relative error of at most 0.025.
Values may be sent and summed in bfloat16 or wider, within the bound.
A program may use at most 128 MiB of HBM per device.

v0:
```python
import jax
import jax.numpy as jnp
from jax import lax
from jax.sharding import PartitionSpec as P

D = 6144
EXPERTS = 8
CAP = 8


epsilon_value = 1e-05


def route_tables(routes, experts, capacity):
    token_rows = routes.shape[0]
    flat_routes = routes.reshape(-1)
    member = (flat_routes[:, None] == jnp.arange(experts, dtype=jnp.int32)[None, :]).astype(
        jnp.int32
    )
    earlier = jnp.cumsum(member, axis=0) - member
    slot_index = jnp.sum(earlier * member, axis=1)
    destination = flat_routes * capacity + slot_index
    table = (
        jnp.arange(experts * capacity, dtype=jnp.int32)[:, None] == destination[None, :]
    ).astype(jnp.bfloat16)
    token_table = jnp.sum(table.reshape(experts * capacity, token_rows, 2), axis=2)
    return (table, token_table)


def expert_backward(inputs, cotangents, w_gate, w_up, w_down):
    gate_pre = jnp.einsum("sjcd,jdh->sjch", inputs, w_gate, preferred_element_type=jnp.float32)
    up_pre = jnp.einsum("sjcd,jdh->sjch", inputs, w_up, preferred_element_type=jnp.float32)
    back_hidden = jnp.einsum(
        "sjcd,jhd->sjch", cotangents, w_down, preferred_element_type=jnp.float32
    )
    sigma = jax.nn.sigmoid(gate_pre)
    grad_gate = (back_hidden * up_pre * sigma * (1.0 + gate_pre * (1.0 - sigma))).astype(
        jnp.bfloat16
    )
    grad_up = (back_hidden * (gate_pre * sigma)).astype(jnp.bfloat16)
    partial_sum = jnp.einsum(
        "sjch,jdh->sjcd", grad_gate, w_gate, preferred_element_type=jnp.float32
    )
    partial_sum = partial_sum + jnp.einsum(
        "sjch,jdh->sjcd", grad_up, w_up, preferred_element_type=jnp.float32
    )
    return partial_sum.astype(jnp.bfloat16)


def local(
    pool,
    prompt_ids,
    tenant,
    lengths,
    routes,
    route_weight,
    cotangent,
    norm_gain,
    w_gate,
    w_up,
    w_down,
):
    token_rows = routes.shape[0]
    feat_dev = cotangent.shape[1]
    local_experts = w_gate.shape[0]
    group_ids = prompt_ids[tenant[0]]
    piece = lax.all_gather(pool, ("dp", "expert"), axis=0, tiled=True)
    lookup = (group_ids[:, None] == jnp.arange(piece.shape[0], dtype=jnp.int32)[None, :]).astype(
        jnp.bfloat16
    )
    row_values = jnp.dot(lookup, piece, preferred_element_type=jnp.float32)
    rows_bf = row_values.astype(jnp.bfloat16)
    live = (jnp.arange(token_rows, dtype=jnp.int32) < lengths[0]).astype(jnp.float32)
    gain_full = norm_gain.astype(jnp.float32)
    gain_shard = lax.dynamic_slice_in_dim(
        gain_full, lax.axis_index("tensor") * feat_dev, feat_dev, 0
    )
    masked = cotangent.astype(jnp.float32) * live[:, None]
    table, token_table = route_tables(routes, EXPERTS, CAP)
    full_rows, full_cot = (
        lax.all_gather(rows_bf, "tensor", axis=1, tiled=True),
        lax.all_gather(cotangent, "tensor", axis=1, tiled=True),
    )
    full_values = full_rows.astype(jnp.float32)
    scale = lax.rsqrt(jnp.mean(full_values * full_values, axis=1) + epsilon_value)
    normed = (full_values * scale[:, None] * gain_full).astype(jnp.bfloat16)
    full_masked = full_cot.astype(jnp.float32) * live[:, None]
    expert_cot = (route_weight[:, :, None] * full_masked[:, None, :]).astype(jnp.bfloat16)
    send_rows = jnp.dot(token_table, normed, preferred_element_type=jnp.float32).astype(
        jnp.bfloat16
    )
    send_cots = jnp.dot(
        table, expert_cot.reshape(token_rows * 2, D), preferred_element_type=jnp.float32
    ).astype(jnp.bfloat16)
    send_rows = send_rows.reshape(EXPERTS, CAP, D)
    send_cots = send_cots.reshape(EXPERTS, CAP, D)
    recv_rows, recv_cots = (
        lax.all_to_all(send_rows, "expert", split_axis=0, concat_axis=0, tiled=True),
        lax.all_to_all(send_cots, "expert", split_axis=0, concat_axis=0, tiled=True),
    )
    all_rows, all_cots = (
        lax.all_gather(recv_rows, "dp", axis=0, tiled=True),
        lax.all_gather(recv_cots, "dp", axis=0, tiled=True),
    )
    sources = all_rows.shape[0] // local_experts
    inputs = all_rows.reshape(sources, local_experts, CAP, D)
    cotangents = all_cots.reshape(sources, local_experts, CAP, D)
    partial_sum = expert_backward(inputs, cotangents, w_gate, w_up, w_down)
    feature_sums = (
        lax.psum_scatter(partial_sum, "tensor", scatter_dimension=3, tiled=True)
        .astype(jnp.float32)
        .astype(jnp.bfloat16)
    )
    feature_sums = feature_sums.reshape(sources * local_experts, CAP, feat_dev)
    group_total = (
        lax.psum_scatter(feature_sums, "dp", scatter_dimension=0, tiled=True)
        .astype(jnp.float32)
        .astype(jnp.bfloat16)
    )
    returned = lax.all_to_all(group_total, "expert", split_axis=0, concat_axis=0, tiled=True)
    returned_flat = returned.reshape(EXPERTS * CAP, feat_dev)
    row_normed_grad = jnp.einsum(
        "sr,sd->rd", token_table, returned_flat, preferred_element_type=jnp.float32
    )
    weighted = row_normed_grad * gain_shard
    row_dot = lax.psum(jnp.sum(weighted * row_values, axis=1), "tensor")
    row_grad = (
        masked
        + scale[:, None] * weighted
        - row_values * (scale * scale * scale * row_dot / D)[:, None]
    )
    pool_rows_dev = pool.shape[0]
    groups = lax.axis_size(("dp", "expert"))
    everywhere = (
        group_ids[:, None] == jnp.arange(pool_rows_dev * groups, dtype=jnp.int32)[None, :]
    ).astype(jnp.float32)
    spread = lax.dot_general(
        everywhere,
        row_grad,
        (((0,), (0,)), ((), ())),
        precision=lax.Precision.HIGHEST,
        preferred_element_type=jnp.float32,
    )
    return lax.psum_scatter(
        spread.astype(jnp.bfloat16), ("dp", "expert"), scatter_dimension=0, tiled=True
    ).astype(jnp.float32)


def solution(mesh):
    placed = (
        P(("dp", "expert"), "tensor"),
        P(),
        P(("dp", "expert")),
        P(("dp", "expert")),
        P(("dp", "expert"), None),
        P(("dp", "expert"), None),
        P(("dp", "expert"), "tensor"),
        P(),
        P("expert", None, ("dp", "tensor")),
        P("expert", None, ("dp", "tensor")),
        P("expert", ("dp", "tensor"), None),
    )
    return jax.shard_map(
        local, mesh=mesh, in_specs=placed, out_specs=P(("dp", "expert"), "tensor"), check_vma=False
    )
```

profile of v0, /device:TPU:1, one launch (start us, length us, event | category | flops | bytes accessed | tf_op | source)
XLA Modules:
  0.0 771.4 jit_solution(4589396887946719970)
XLA Ops:
  7.3 47.5 %all_gather.15 = bf16[512,384]{1,0:T(8,128)(2,1)S(1)} all-gather(bf16[16,384]{1,0:T(8,128)(2,1)} %param.11), channel_id=1, replica_groups=mesh['dp'=4,'expert'=8,'tensor'=16] {'dp','expert'}, dimensions={0}, use_global_device_ids=true | all-gather | bytes 405504 | tf_op jit(solution)/shard_map/all_gather | solution.py:67
  55.9 50.4 %all_gather.16 = bf16[24,6144]{1,0:T(8,128)(2,1)S(1)} all-gather(bf16[24,384]{1,0:T(8,128)(2,1)S(1)} %get-tuple-element.5), channel_id=1, replica_groups=mesh['dp'=4,'expert'=8,'tensor'=16] {'tensor'}, dimensions={1}, use_global_device_ids=true | all-gather | bytes 313344 | tf_op jit(solution)/shard_map/all_gather | solution.py:81
  109.4 10.7 %all-to-all-start.1 = ((bf16[8,8,6144]{2,1,0:T(8,128)(2,1)}), bf16[8,8,6144]{2,1,0:T(8,128)(2,1)S(1)}, u32[]{:S(2)}, u32[]{:S(2)}) async-start(bf16[8,8,6144]{2,1,0:T(8,128)(2,1)} %fusion.3), calls=%async_computation.1 | async-start | bytes 1572864 | tf_op jit(solution)/shard_map/all_to_all | solution.py:98
  120.8 19.7 %all-to-all-done.1 = bf16[8,8,6144]{2,1,0:T(8,128)(2,1)S(1)} async-done(((bf16[8,8,6144]{2,1,0:T(8,128)(2,1)}), bf16[8,8,6144]{2,1,0:T(8,128)(2,1)S(1)}, u32[]{:S(2)}, u32[]{:S(2)}) %all-to-all-start.1) | async-done | bytes 786464 | tf_op jit(solution)/shard_map/all_to_all | solution.py:98
  141.4 42.2 %all_gather.17 = bf16[24,6144]{1,0:T(8,128)(2,1)S(1)} all-gather(bf16[24,384]{1,0:T(8,128)(2,1)S(1)} %copy-done.4), channel_id=1, replica_groups=mesh['dp'=4,'expert'=8,'tensor'=16] {'tensor'}, dimensions={1}, use_global_device_ids=true | all-gather | bytes 313344 | tf_op jit(solution)/shard_map/all_gather | solution.py:82
  183.7 1.6 mul.141
  185.4 2.1 mul.142
  188.1 29.9 %all_to_all.15 = bf16[8,8,6144]{2,1,0:T(8,128)(2,1)} all-to-all(bf16[8,8,6144]{2,1,0:T(8,128)(2,1)S(1)} %fusion.2), channel_id=1, replica_groups=mesh['dp'=4,'expert'=8,'tensor'=16] {'expert'}, dimensions={0} | all-to-all | bytes 1572864 | tf_op jit(solution)/shard_map/all_to_all | solution.py:99
  218.1 2.9 fusion.28
  221.0 36.2 %all-gather.3.cloned.1.call-done = bf16[32,8,6144]{2,1,0:T(8,128)(2,1)} async-done(((bf16[8,8,6144]{2,1,0:T(8,128)(2,1)}), bf16[32,8,6144]{2,1,0:T(8,128)(2,1)}) %all-gather.3.cloned.1.call-update) | async-done | bytes 3145744 | tf_op jit(solution)/shard_map/all_gather | solution.py:103
  257.2 3.3 fusion.13
  260.5 8.0 %fusion.4 = f32[32,8,6144]{2,1,0:T(8,128)} fusion(bf16[1,6144,128]{2,1,0:T(8,128)(2,1)S(1)} %copy-done.2, f32[32,1,8,128]{3,2,0,1:T(8,128)S(1)} %fusion.13, bf16[32,8,6144]{2,1,0:T(8,128)(2,1)} %all-gather.5.cloned.1.call-done, bf16[1,6144,128]{2,1,0:T(8,128)(2,1)S(1)} %copy-done, f32[32,1,8,128]{3,2,0,1:T(8,128)S(1)} %fusion.28), kind=kOutput, calls=%fused_computation.7 | convolution fusion | flops 805634048 | bytes 12845056 | tf_op jit(solution)/shard_map/sjch,jdh->sjcd/dot_general | solution.py:41
  268.5 5.4 fusion.1
  273.9 39.6 %copy.32 = bf16[32,1,8,6144]{2,0,1,3:T(8,128)(2,1)} copy(bf16[32,1,8,6144]{3,2,0,1:T(8,128)(2,1)} %fusion.1) | data formatting | bytes 6291456
  313.5 69.9 %reshape.96 = bf16[6144,256]{1,0:T(8,128)(2,1)} reshape(bf16[6144,1,32,8]{3,2,1,0:T(8,128)(2,1)} %bitcast.104) | data formatting | bytes 6291456
  383.7 141.5 %reduce-scatter.10.cloned.1.call-done = bf16[384,256]{1,0:T(8,128)(2,1)} async-done(((bf16[6144,256]{1,0:T(8,128)(2,1)}), bf16[384,256]{1,0:T(8,128)(2,1)}) %reduce-scatter.10.cloned.1.call-update) | async-done | bytes 196624
  525.2 5.6 reshape.97
  530.8 5.1 copy.33
  536.0 22.2 %reduce-scatter.6.cloned.1.call-done = bf16[8,8,384]{2,1,0:T(8,128)(2,1)} async-done(((bf16[32,8,384]{2,1,0:T(8,128)(2,1)}), bf16[8,8,384]{2,1,0:T(8,128)(2,1)}) %reduce-scatter.6.cloned.1.call-update) | async-done | bytes 49168 | tf_op jit(solution)/shard_map/reduce_scatter | solution.py:116
  558.2 7.7 all-to-all-start.2
  565.9 4.9 all-to-all-done.2
  571.1 46.1 %psum.7 = f32[24]{0:T(128)S(1)} all-reduce(f32[24]{0:T(128)S(1)} %get-tuple-element.7), channel_id=1, replica_groups=mesh['dp'=4,'expert'=8,'tensor'=16] {'tensor'}, use_global_device_ids=true, to_apply=%region_7.8 | all-reduce | flops 24 | bytes 192 | tf_op jit(solution)/shard_map/psum | solution.py:126
  617.2 1.3 convolution_convert_fusion.2
  618.5 145.0 %reduce-scatter.8.cloned.1.call-done = bf16[16,384]{1,0:T(8,128)(2,1)} async-done(((bf16[512,384]{1,0:T(8,128)(2,1)}), bf16[16,384]{1,0:T(8,128)(2,1)}) %reduce-scatter.8.cloned.1.call-update) | async-done | bytes 12304 | tf_op jit(solution)/shard_map/reduce_scatter | solution.py:144
  (52 shorter events, 7.8 us)
Async XLA Ops:
  6.5 254.0 %copy-start = (bf16[1,6144,128]{2,1,0:T(8,128)(2,1)S(1)}, bf16[1,6144,128]{2,1,0:T(8,128)(2,1)}, u32[]{:S(2)}) copy-start(bf16[1,6144,128]{2,1,0:T(8,128)(2,1)} %param.20) | copy-start | bytes 4718596
  6.5 101.4 %copy-start.6 = (s32[24,2]{0,1:T(2,128)S(1)}, s32[24,2]{0,1:T(2,128)}, u32[]{:S(2)}) copy-start(s32[24,2]{0,1:T(2,128)} %param.15) | copy-start | bytes 580
  6.5 101.5 %copy-start.5 = (bf16[6144]{0:T(1024)(128)(2,1)S(1)}, bf16[6144]{0:T(1024)(128)(2,1)}, u32[]{:S(2)}) copy-start(bf16[6144]{0:T(1024)(128)(2,1)} %param.18) | copy-start | bytes 36868
  108.1 33.3 %copy-start.4 = (bf16[24,384]{1,0:T(8,128)(2,1)S(1)}, bf16[24,384]{1,0:T(8,128)(2,1)}, u32[]{:S(2)}) copy-start(bf16[24,384]{1,0:T(8,128)(2,1)} %param.17) | copy-start | bytes 55300
  109.4 31.1 %all-to-all-start.1 = ((bf16[8,8,6144]{2,1,0:T(8,128)(2,1)}), bf16[8,8,6144]{2,1,0:T(8,128)(2,1)S(1)}, u32[]{:S(2)}, u32[]{:S(2)}) async-start(bf16[8,8,6144]{2,1,0:T(8,128)(2,1)} %fusion.3), calls=%async_computation.1 | async-start | bytes 1572864 | tf_op jit(solution)/shard_map/all_to_all | solution.py:98
  120.1 98.0 %all-gather.5.cloned.1.call-start = ((), (), s32[]{:S(2)}) async-start(), calls=%async_computation.7 | async-start | bytes 3932160 | tf_op jit(solution)/shard_map/all_gather | solution.py:102
  140.4 0.9 copy-start.3
  141.3 115.9 %all-gather.3.cloned.1.call-start = ((), (), s32[]{:S(2)}) async-start(), calls=%async_computation.6 | async-start | bytes 3932160 | tf_op jit(solution)/shard_map/all_gather | solution.py:103
  185.4 2.1 copy-start.7
  188.1 30.0 %copy-start.2 = (bf16[1,6144,128]{2,1,0:T(8,128)(2,1)S(1)}, bf16[1,6144,128]{2,1,0:T(8,128)(2,1)}, u32[]{:S(2)}) copy-start(bf16[1,6144,128]{2,1,0:T(8,128)(2,1)} %param.19) | copy-start | bytes 4718596
  218.0 307.2 %reduce-scatter.10.cloned.1.call-start = ((), (), s32[]{:S(2)}) async-start(), calls=%async_computation.10 | async-start | bytes 3342336
  383.5 174.7 %reduce-scatter.6.cloned.1.call-start = ((), (), s32[]{:S(2)}) async-start(), calls=%async_computation.8 | async-start | bytes 245760 | tf_op jit(solution)/shard_map/reduce_scatter | solution.py:116
  530.8 234.1 %copy-start.1 = (bf16[1,6144,128]{2,1,0:T(8,128)(2,1)S(1)}, bf16[1,6144,128]{2,1,0:T(8,128)(2,1)}, u32[]{:S(2)}) copy-start(bf16[1,6144,128]{2,1,0:T(8,128)(2,1)} %param.20) | copy-start | bytes 4718596
  558.2 12.7 %all-to-all-start.2 = ((bf16[8,8,384]{2,1,0:T(8,128)(2,1)}), bf16[8,8,384]{2,1,0:T(8,128)(2,1)S(1)}, u32[]{:S(2)}, u32[]{:S(2)}) async-start(bf16[8,8,384]{2,1,0:T(8,128)(2,1)} %reduce-scatter.6.cloned.1.call-done), calls=%async_computation.3 | async-start | bytes 98304 | tf_op jit(solution)/shard_map/all_to_all | solution.py:120
  565.9 197.7 %reduce-scatter.8.cloned.1.call-start = ((), (), s32[]{:S(2)}) async-start(), calls=%async_computation.9 | async-start | bytes 405504 | tf_op jit(solution)/shard_map/reduce_scatter | solution.py:144
Sparse Core Ops, SparseCore 0:
  141.5 37.8 all-gather.4
  218.2 38.9 all-gather.2
  383.6 141.5 reduce-scatter.9
  536.1 22.0 reduce-scatter.5
  618.7 144.8 reduce-scatter.7
where the time goes:
time: 778 us; the launch traced here: 771 us
  waiting for transfers between devices  370 us (48%)
  blocking collectives  216 us (28%)
  local copies, waits for them, and re-layouts  127 us (16%)
  matrix products  23.1 us (3%)
  starting transfers between devices  18.7 us (2%)
  between operations  14.7 us (2%)
    reduce_scatter x1, waiting for transfers between devices, local(): lax.psum_scatter(spread.astype(jnp.bfloat16), ('dp', 'expert'), scatter_d...  145 us
    unnamed x6, waiting for transfers between devices  142 us
    unnamed x22, local copies, waits for them, and re-layouts  122 us
    all_gather x1, blocking collectives, local(): lax.all_gather(rows_bf, 'tensor', axis=1, tiled=True)  50.4 us
    all_gather x1, blocking collectives, local(): piece = lax.all_gather(pool, ('dp', 'expert'), axis=0, tiled=True)  47.5 us
    psum x1, blocking collectives, local(): row_dot = lax.psum(jnp.sum(weighted * row_values, axis=1), 'tensor')  46.1 us
    all_gather x1, blocking collectives, local(): lax.all_gather(cotangent, 'tensor', axis=1, tiled=True)  42.2 us
    all_gather x1, waiting for transfers between devices, local(): lax.all_gather(recv_cots, 'dp', axis=0, tiled=True)  36.2 us
  transfers between devices with their start and end apart: 7, of which 6 were waited for; matrix products, arithmetic and copies ran while one was open for 1% of the time, Pallas kernels for 0%

commit v1 on v0

v1 whole, which is shorter than its diff:
```python
import functools
import heapq

import jax
import jax.numpy as jnp
from jax import lax
from jax.experimental import pallas as pl
from jax.experimental.pallas import tpu as pltpu
from jax.sharding import PartitionSpec as P

D = 6144
EPSILON = 1e-05
MESH = pl.DeviceIdType.MESH
F32, BF16 = jnp.float32, jnp.bfloat16
POOL_ROWS, COT_ROWS, PROMPT = 32, 48, 24
TOKENS = 768
GROUP_ORDER = (2, 1, 3, 0)
NT = (((1,), (1,)), ((), ()))
KEEP = slice(None)


class Net:
    def __init__(self, send_sems, recv_sems):
        self.x = lax.axis_index("dp")
        expert = lax.axis_index("expert")
        tensor = lax.axis_index("tensor")
        self.zl, self.c = expert // 2, expert % 2
        self.zh, self.y = tensor // 4, tensor % 4
        self.z = self.zh * 4 + self.zl
        self.send_sems, self.recv_sems = send_sems, recv_sems
        self.slots = {}
        self.sent = []

    def device(self, x=None, y=None, z=None, c=None):
        x = self.x if x is None else x
        y = self.y if y is None else y
        z = self.z if z is None else z
        c = self.c if c is None else c
        return (x, (z % 4) * 2 + c, (z // 4) * 4 + y)

    def copy(self, key, src, dst, device):
        slot = self.slots.setdefault(key, len(self.slots))
        return pltpu.make_async_remote_copy(
            src_ref=src,
            dst_ref=dst,
            send_sem=self.send_sems.at[slot],
            recv_sem=self.recv_sems.at[slot],
            device_id=device,
            device_id_type=MESH,
        )

    def start(self, key, src, dst, device):
        copy = self.copy(key, src, dst, device)
        copy.start()
        self.sent.append(copy)

    def wait(self, key, dst):
        self.copy(key, dst, dst, self.device(c=1 - self.c)).wait_recv()

    def drain(self):
        for copy in self.sent:
            copy.wait_send()
        self.sent = []


def kind(core, o):
    return "cot" if (core + o) % 2 == 0 else "pool"


ORDERS = ("zyx", "xzy", "yxz")


def region(net, o, done, axis=None, pos=None):
    z = pos if axis == "z" else net.z
    zh, zl = (KEEP, KEEP) if "z" in done else (z // 4, z % 4)
    y = KEEP if "y" in done else (pos if axis == "y" else net.y)
    x = KEEP if "x" in done else (pos if axis == "x" else net.x)
    return (o, zh, y, x, zl)


def gather_order(net, core, o, buf):
    order = ORDERS[o]
    now = 2.0
    done = ""
    for phase, axis in enumerate(order):
        size = 16 if axis == "z" else 4
        me = {"x": net.x, "y": net.y, "z": net.z}[axis]
        last = phase == 2

        def unit(pos, done=done, axis=axis):
            return buf.at[region(net, o, done, axis, pos)]

        def send(step, pos, key, unit=unit, axis=axis, size=size, me=me):
            there = net.device(**{axis: (me + step) % size})
            net.start((o, phase, key), unit(pos), unit(pos), there)

        def to_partner(pos, name, unit=unit):
            net.start((o, "partner", name), unit(pos), unit(pos), net.device(c=1 - net.c))

        if last:
            to_partner(me, 0)
        if not last and axis != "z":
            for step in (2, 1, 3):
                send(step, me, step)
            now += 3.0 if phase == 0 else 4.5
            for step in (1, 3, 2):
                yield now
                net.wait((o, phase, step), unit((me - step) % size))
        else:
            right, left = (size // 2, size // 2 - 1) if core == 0 else (size // 2 - 1, size // 2)
            if axis == "z":
                tick = 3.4 if last else 2.2
            else:
                tick = 9.0
            send(1, me, ("right", 1))
            send(-1, me, ("left", 1))
            for step in range(1, size // 2 + 1):
                now += tick
                for name, sign, count in (("right", 1, right), ("left", -1, left)):
                    if step > count:
                        continue
                    yield now
                    pos = (me - sign * step) % size
                    net.wait((o, phase, (name, step)), unit(pos))
                    if step < count:
                        send(sign, pos, (name, step + 1))
                    if last:
                        to_partner(pos, sign * step)
        done = done + axis


def partner_names(core, o):
    size = 16 if ORDERS[o][2] == "z" else 4
    right, left = (size // 2, size // 2 - 1) if core == 0 else (size // 2 - 1, size // 2)
    names = [0]
    for step in range(1, size // 2 + 1):
        names += [step] if step <= right else []
        names += [-step] if step <= left else []
    return names


def facts_stages(net, facts_ref, facts_got, facts_sum):
    net.start(("facts", 0), facts_ref, facts_got.at[0], net.device(c=1 - net.c))
    yield 3.0
    net.wait(("facts", 0), facts_got.at[0])
    facts_sum[0] = facts_ref[...] + facts_got[0]
    for j in (1, 2, 3):
        there = net.device(z=net.zh * 4 + (net.zl + j) % 4)
        net.start(("facts", j), facts_sum.at[0], facts_got.at[j], there)
    yield 8.5
    for j in (1, 2, 3):
        net.wait(("facts", j), facts_got.at[j])
    facts_sum[1] = facts_sum[0] + facts_got[1] + facts_got[2] + facts_got[3]
    for j in (1, 2, 3):
        there = net.device(x=(net.x + j) % 4)
        net.start(("facts", 3 + j), facts_sum.at[1], facts_got.at[3 + j], there)
    yield 14.5
    for j in (1, 2, 3):
        net.wait(("facts", 3 + j), facts_got.at[3 + j])
    facts_sum[2] = facts_sum[1] + facts_got[4] + facts_got[5] + facts_got[6]


def run_all(tasks):
    heap = []
    for number, task in enumerate(tasks):
        time = next(task, None)
        if time is not None:
            heapq.heappush(heap, (time, number, task))
    while heap:
        _, number, task = heapq.heappop(heap)
        time = next(task, None)
        if time is not None:
            heapq.heappush(heap, (time, number, task))


def gather(net, core, pool_ref, cot_ref, facts_ref, bufs, padded, landed, facts_got, facts_sum):
    partner = net.device(c=1 - net.c)
    here = (net.zh, net.y, net.x, net.zl)
    own_rows = pl.ds(16 * core, 16)
    for o in range(3):
        columns = slice(o * 128, (o + 1) * 128)
        if kind(core, o) == "cot":
            dst = bufs["pool"].at[(o,) + here + (own_rows,)]
            net.start(("swap", o), pool_ref.at[:, pl.ds(o * 128, 128)], dst, partner)
        else:
            block = cot_ref[:, columns].astype(F32)
            padded[o] = jnp.concatenate([block, jnp.zeros((8, 128), F32)], axis=0).astype(BF16)
            net.start(("swap", o), padded.at[o], landed.at[o], partner)
    for o in range(3):
        columns = slice(o * 128, (o + 1) * 128)
        if kind(core, o) == "pool":
            bufs["pool"][(o,) + here + (own_rows,)] = pool_ref[:, columns]
            net.wait(("swap", o), bufs["pool"].at[(o,) + here + (pl.ds(16 * (1 - core), 16),)])
        else:
            net.wait(("swap", o), landed.at[o])
            own = cot_ref[:, columns].astype(F32)
            other = landed[o].astype(F32)[:PROMPT]
            pair = [own, other] if core == 0 else [other, own]
            bufs["cot"][(o,) + here] = jnp.concatenate(pair, axis=0).astype(BF16)
    run_all(
        [gather_order(net, core, o, bufs[kind(core, o)]) for o in range(3)]
        + [facts_stages(net, facts_ref, facts_got, facts_sum)]
    )
    for o in range(3):
        axis = ORDERS[o][2]
        size = 16 if axis == "z" else 4
        me = {"x": net.x, "y": net.y, "z": net.z}[axis]
        buf = bufs[kind(1 - core, o)]
        for name in partner_names(1 - core, o):
            unit = buf.at[region(net, o, ORDERS[o][:2], axis, (me - name) % size)]
            net.wait((o, "partner", name), unit)
    net.drain()


def kernel(
    pool_ref,
    cot_ref,
    facts_ref,
    gain_ref,
    own_gain_ref,
    w_gate_hbm,
    w_up_hbm,
    w_down_hbm,
    out_ref,
    pool_buf,
    cot_buf,
    w_in,
    w_out,
    padded,
    landed,
    facts_got,
    facts_sum,
    hidden,
    back,
    squares,
    scales,
    grads,
    part_out,
    part_in,
    sums,
    first_a,
    first_b,
    mid_a,
    mid_b,
    second_a,
    second_b,
    plane,
    last,
    dot_own,
    dot_pair,
    dot_sum,
    dot_x,
    dot_y,
    dot_z,
    weight_sems,
    send_sems,
    recv_sems,
):
    net = Net(send_sems, recv_sems)
    partner = net.device(c=1 - net.c)
    loads = [
        pltpu.make_async_copy(w_gate_hbm, w_in.at[:, :, pl.ds(0, 128)], weight_sems.at[0]),
        pltpu.make_async_copy(w_up_hbm, w_in.at[:, :, pl.ds(128, 128)], weight_sems.at[1]),
        pltpu.make_async_copy(w_down_hbm, w_out, weight_sems.at[2]),
    ]
    for load in loads:
        load.start()

    barrier = pltpu.get_barrier_semaphore()
    peers = [partner]
    for j in (1, 2, 3):
        peers += [net.device(x=(net.x + j) % 4), net.device(y=(net.y + j) % 4)]
    peers += [net.device(z=(net.z + j) % 16) for j in range(1, 16)]
    for peer in peers:
        pl.semaphore_signal(barrier, inc=1, device_id=peer, device_id_type=MESH)
    pl.semaphore_wait(barrier, len(peers))

    bufs = {"pool": pool_buf, "cot": cot_buf}
    for core in range(2):

        @pl.when(net.c == core)
        def _():
            branch = Net(send_sems, recv_sems)
            branch.slots = net.slots
            gather(
                branch, core, pool_ref, cot_ref, facts_ref, bufs, padded, landed, facts_got, facts_sum
            )

    for load in loads:
        load.wait()

    hidden[...] = jnp.zeros_like(hidden)
    back[...] = jnp.zeros_like(back)
    squares[...] = jnp.zeros_like(squares)
    for o in range(3):

        def columns_step(zh, carry, o=o):
            blocks = [(zh * 4 + y) * 3 + o for y in range(4)]
            normed = []
            square = None
            for y in range(4):
                value = pool_buf[o, zh, y].reshape(16 * POOL_ROWS, 128).astype(F32)
                square = value * value if square is None else square + value * value
                normed.append((value * gain_ref[pl.ds(blocks[y], 1), :]).astype(BF16))
            squares[...] += square
            weights = jnp.concatenate([w_in[b] for b in blocks], axis=0)
            hidden[...] += jnp.dot(
                jnp.concatenate(normed, axis=1), weights, preferred_element_type=F32
            )
            cots = jnp.concatenate(
                [cot_buf[o, zh, y].reshape(TOKENS, 128) for y in range(4)], axis=1
            )
            downs = jnp.concatenate(
                [w_out[:, pl.ds(pl.multiple_of(b * 128, 128), 128)] for b in blocks], axis=1
            )
            back[...] += lax.dot_general(cots, downs, NT, preferred_element_type=F32)
            return carry

        lax.fori_loop(0, 4, columns_step, 0)

    ids = facts_sum[2, 0:1]
    live = facts_sum[2, 1:2]
    expert = (net.zl * 2 + net.c).astype(F32)
    weight = jnp.where(facts_sum[2, 2:3] == expert, facts_sum[2, 4:5], 0.0) + jnp.where(
        facts_sum[2, 3:4] == expert, facts_sum[2, 5:6], 0.0
    )
    back_all = back[...]
    back_hi = back_all.astype(BF16)
    back_lo = (back_all - back_hi.astype(F32)).astype(BF16)

    def rows_step(i, carry):
        rows = pl.ds(pl.multiple_of(i * 128, 128), 128)
        number = (lax.broadcasted_iota(jnp.int32, (128, 1), 0) + i * 128).astype(F32)
        place = jnp.where(ids == number, weight, 0.0)
        place_hi = place.astype(BF16)
        place_lo = (place - place_hi.astype(F32)).astype(BF16)
        got = jnp.dot(place_hi, back_hi, preferred_element_type=F32)
        got += jnp.dot(place_hi, back_lo, preferred_element_type=F32)
        got += jnp.dot(place_lo, back_hi, preferred_element_type=F32)
        scale = lax.rsqrt(jnp.sum(squares[rows], axis=1, keepdims=True) / D + EPSILON)
        scales[rows] = jnp.broadcast_to(scale, (128, 128))
        raw_gate, raw_up = hidden[rows, 0:128], hidden[rows, 128:256]
        gate, up = raw_gate * scale, raw_up * scale
        sigma = jax.nn.sigmoid(gate)
        grad_gate = got * up * sigma * (1.0 + gate * (1.0 - sigma))
        grad_up = got * (gate * sigma)
        both = jnp.concatenate([grad_gate, grad_up], axis=1).astype(BF16).reshape(4, 2, 16, 256)
        half = pl.ds(pl.multiple_of(i * 64, 64), 64)
        grads[0, half] = both[:, 0].reshape(64, 256)
        grads[1, half] = both[:, 1].reshape(64, 256)
        product = grad_gate * raw_gate + grad_up * raw_up
        dot_own[:, rows] = lax.dot_general(
            jnp.ones((8, 128), F32),
            product,
            NT,
            precision=lax.Precision.HIGHEST,
            preferred_element_type=F32,
        )
        return carry

    lax.fori_loop(0, 4, rows_step, 0)

    def product(parity, zh, y):
        weights = jnp.concatenate([w_in[(zh * 4 + y) * 3 + o] for o in range(3)], axis=0)
        return lax.dot_general(grads[parity], weights, NT, preferred_element_type=F32)

    net.start("dot_pair", dot_own, dot_pair, partner)
    spots = [(net.zh + step) % 4 for step in GROUP_ORDER]
    for g, zh in enumerate(spots):

        def other_step(y, carry, zh=zh):
            part_out[zh, y] = product(1 - net.c, zh, y).astype(BF16).reshape(4, 4, 16, 384)
            return carry

        lax.fori_loop(0, 4, other_step, 0)
        net.start(("part", g), part_out.at[zh], part_in.at[zh], partner)

    lanes = [pl.ds(pl.multiple_of((net.x + j) % 4 * 128, 128), 128) for j in range(4)]

    def begin(g):
        zh = spots[g]
        net.wait(("part", g), part_in.at[zh])

        def own_step(y, carry):
            total = product(net.c, zh, y).reshape(4, 4, 16, 384) + part_in[zh, y].astype(F32)
            sums[zh, y] = total.astype(BF16)
            return carry

        lax.fori_loop(0, 4, own_step, 0)
        for j in (2, 1, 3):
            x, y = (net.x + j) % 4, (net.y + j) % 4
            net.start(
                ("a1", g, j), sums.at[zh, :, x, pl.ds(0, 2)], first_a.at[g, j - 1], net.device(x=x)
            )
            net.start(
                ("b1", g, j), sums.at[zh, y, :, pl.ds(2, 2)], first_b.at[g, j - 1], net.device(y=y)
            )

    def middle(g):
        zh = spots[g]
        for j in (1, 2, 3):
            net.wait(("a1", g, j), first_a.at[g, j - 1])
            net.wait(("b1", g, j), first_b.at[g, j - 1])
        own_a = sums[zh, :, net.x, 0:2].astype(F32)
        own_b = sums[zh, net.y, :, 2:4].astype(F32)
        for j in range(3):
            own_a += first_a[g, j].astype(F32)
            own_b += first_b[g, j].astype(F32)
        mid_a[g] = own_a.astype(BF16)
        mid_b[g] = own_b.astype(BF16)
        for j in (2, 1, 3):
            x, y = (net.x + j) % 4, (net.y + j) % 4
            net.start(("a2", g, j), mid_a.at[g, y], second_a.at[g, j - 1], net.device(y=y))
            net.start(("b2", g, j), mid_b.at[g, x], second_b.at[g, j - 1], net.device(x=x))

    def finish(g):
        step = GROUP_ORDER[g]
        for j in (1, 2, 3):
            net.wait(("a2", g, j), second_a.at[g, j - 1])
            net.wait(("b2", g, j), second_b.at[g, j - 1])
        own_a = mid_a[g, net.y].astype(F32)
        own_b = mid_b[g, net.x].astype(F32)
        for j in range(3):
            own_a += second_a[g, j].astype(F32)
            own_b += second_b[g, j].astype(F32)
        plane[g, 0:2] = own_a.astype(BF16)
        plane[g, 2:4] = own_b.astype(BF16)
        for j in range(4):
            if step == 0 and j == 0:
                continue
            zl = (net.zl + j) % 4
            slot = step * 4 + j
            net.start(
                ("z", slot), plane.at[g, zl], last.at[slot], net.device(z=spots[g] * 4 + zl)
            )

    def dot_one():
        net.wait("dot_pair", dot_pair)
        dot_sum[...] = dot_own[...] + dot_pair[...]
        for j in (1, 2, 3):
            net.start(
                ("dot_x", j), dot_sum.at[:, lanes[j]], dot_x.at[j], net.device(x=(net.x + j) % 4)
            )

    def dot_two():
        for j in (1, 2, 3):
            net.wait(("dot_x", j), dot_x.at[j])
        dot_y[0] = dot_sum[:, lanes[0]] + dot_x[1] + dot_x[2] + dot_x[3]
        for j in (1, 2, 3):
            net.start(("dot_y", j), dot_y.at[0], dot_y.at[j], net.device(y=(net.y + j) % 4))

    def dot_three():
        for j in (1, 2, 3):
            net.wait(("dot_y", j), dot_y.at[j])
        dot_z[0] = dot_y[0] + dot_y[1] + dot_y[2] + dot_y[3]
        for j in range(1, 16):
            net.start(("dot_z", j), dot_z.at[0], dot_z.at[j], net.device(z=(net.z + j) % 16))

    begin(0)
    dot_one()
    begin(1)
    middle(0)
    dot_two()
    begin(2)
    middle(1)
    dot_three()
    finish(0)
    begin(3)
    middle(2)
    finish(1)

    first = ((net.x * 4 + net.zl) * 2 + net.c) * 16
    own_number = (lax.broadcasted_iota(jnp.int32, (16, 1), 0) + first).astype(F32)
    own_place = jnp.where(ids == own_number, live, 0.0).astype(BF16)
    direct = jnp.concatenate(
        [
            jnp.dot(
                own_place,
                cot_buf[o, net.zh, net.y].reshape(TOKENS, 128),
                preferred_element_type=F32,
            )
            for o in range(3)
        ],
        axis=1,
    )

    middle(3)
    finish(2)
    finish(3)

    for j in range(1, 16):
        net.wait(("dot_z", j), dot_z.at[j])
    dots = dot_z[0]
    for j in range(1, 16):
        dots += dot_z[j]
    own_lane = (net.zl * 2 + net.c) * 16 + lax.broadcasted_iota(jnp.int32, (16, 128), 0)
    picked = jnp.where(lax.broadcasted_iota(jnp.int32, (16, 128), 1) == own_lane, dots[0:1], 0.0)
    own_dot = jnp.sum(picked, axis=1, keepdims=True)
    scale = scales[pl.ds(pl.multiple_of(first, 16), 16), 0:1]
    factor = scale * scale * scale * own_dot / D

    total = plane[3, net.zl].astype(F32)
    for step in GROUP_ORDER:
        for j in range(4):
            slot = step * 4 + j
            if slot > 0:
                net.wait(("z", slot), last.at[slot])
                total += last[slot].astype(F32)
    out_ref[...] = (
        direct + scale * own_gain_ref[...] * total - pool_ref[...].astype(F32) * factor
    )
    net.drain()


def local(
    pool,
    prompt_ids,
    tenant,
    lengths,
    routes,
    route_weight,
    cotangent,
    norm_gain,
    w_gate,
    w_up,
    w_down,
):
    sequence = lax.axis_index(("dp", "expert"))
    ids = prompt_ids[tenant[0]]
    live = (jnp.arange(PROMPT, dtype=jnp.int32) < lengths[0]).astype(F32)
    facts = jnp.concatenate(
        [
            ids[None].astype(F32),
            live[None],
            routes.T.astype(F32),
            route_weight.T * live[None],
            jnp.zeros((2, PROMPT), F32),
        ],
        axis=0,
    )
    facts = lax.dynamic_update_slice(
        jnp.zeros((8, TOKENS), F32), facts, (0, sequence * PROMPT)
    )
    gain = norm_gain.astype(F32).reshape(48, 128)
    own_gain = lax.dynamic_slice_in_dim(
        norm_gain.astype(F32), lax.axis_index("tensor") * 384, 384, 0
    ).reshape(1, 384)
    vmem = pl.BlockSpec(memory_space=pltpu.VMEM)
    hbm = pl.BlockSpec(memory_space=pl.ANY)
    sums_shape = pltpu.VMEM((4, 4, 4, 4, 16, 384), BF16)
    copies = 200
    return pl.pallas_call(
        kernel,
        out_shape=jax.ShapeDtypeStruct((16, 384), F32),
        in_specs=[vmem] * 5 + [hbm] * 3,
        out_specs=vmem,
        scratch_shapes=[
            pltpu.VMEM((3, 4, 4, 4, 4, POOL_ROWS, 128), BF16),
            pltpu.VMEM((3, 4, 4, 4, 4, COT_ROWS, 128), BF16),
            pltpu.VMEM((48, 128, 256), BF16),
            pltpu.VMEM((128, D), BF16),
            pltpu.VMEM((3, 32, 128), BF16),
            pltpu.VMEM((3, 32, 128), BF16),
            pltpu.VMEM((7, 8, TOKENS), F32),
            pltpu.VMEM((3, 8, TOKENS), F32),
            pltpu.VMEM((512, 256), F32),
            pltpu.VMEM((TOKENS, 128), F32),
            pltpu.VMEM((512, 128), F32),
            pltpu.VMEM((512, 128), F32),
            pltpu.VMEM((2, 256, 256), BF16),
            sums_shape,
            sums_shape,
            sums_shape,
            pltpu.VMEM((4, 3, 4, 2, 16, 384), BF16),
            pltpu.VMEM((4, 3, 4, 2, 16, 384), BF16),
            pltpu.VMEM((4, 4, 2, 16, 384), BF16),
            pltpu.VMEM((4, 4, 2, 16, 384), BF16),
            pltpu.VMEM((4, 3, 2, 16, 384), BF16),
            pltpu.VMEM((4, 3, 2, 16, 384), BF16),
            pltpu.VMEM((4, 4, 16, 384), BF16),
            pltpu.VMEM((16, 16, 384), BF16),
            pltpu.VMEM((8, 512), F32),
            pltpu.VMEM((8, 512), F32),
            pltpu.VMEM((8, 512), F32),
            pltpu.VMEM((4, 8, 128), F32),
            pltpu.VMEM((4, 8, 128), F32),
            pltpu.VMEM((16, 8, 128), F32),
            pltpu.SemaphoreType.DMA((3,)),
            pltpu.SemaphoreType.DMA((copies,)),
            pltpu.SemaphoreType.DMA((copies,)),
        ],
        compiler_params=pltpu.CompilerParams(
            collective_id=0, has_side_effects=True, vmem_limit_bytes=56 * 2**20
        ),
        name="moe_backward",
    )(
        pool,
        cotangent,
        facts,
        gain,
        own_gain,
        w_gate.reshape(48, 128, 128),
        w_up.reshape(48, 128, 128),
        w_down[0],
    )


def solution(mesh):
    placed = (
        P(("dp", "expert"), "tensor"),
        P(),
        P(("dp", "expert")),
        P(("dp", "expert")),
        P(("dp", "expert"), None),
        P(("dp", "expert"), None),
        P(("dp", "expert"), "tensor"),
        P(),
        P("expert", None, ("dp", "tensor")),
        P("expert", None, ("dp", "tensor")),
        P("expert", ("dp", "tensor"), None),
    )
    return jax.shard_map(
        local, mesh=mesh, in_specs=placed, out_specs=P(("dp", "expert"), "tensor"), check_vma=False
    )
```

time: 778 us -> 142 us (0.18)
  waiting for transfers between devices: 370 us -> 0 us
  blocking collectives: 216 us -> 0 us
  Pallas kernels: 0 us -> 135 us
  local copies, waits for them, and re-layouts: 127 us -> 3.31 us
  matrix products: 23.1 us -> 0 us
  starting transfers between devices: 18.7 us -> 0 us
  between operations: 14.7 us -> 1.35 us
    reduce_scatter x2 -> x0, waiting for transfers between devices: 167 us -> none  [the longest x1 145 us: local(): lax.psum_scatter(spread.astype(jnp.bfloat16), ('dp', 'expert'), scatter_d...]
    unnamed x6 -> x0, waiting for transfers between devices: 142 us -> none
    all_gather x3 -> x0, blocking collectives: 140 us -> none  [the longest x1 50.4 us: local(): lax.all_gather(rows_bf, 'tensor', axis=1, tiled=True)]
    pallas_call x0 -> x1, Pallas kernels: none -> 135 us  [local(): pl.pallas_call(kernel, out_shape=jax.ShapeDtypeStruct((16, 384), F32), in...]
    unnamed x22 -> x6, local copies, waits for them, and re-layouts: 122 us -> 1.52 us
    psum x1 -> x0, blocking collectives: 46.1 us -> none  [local(): row_dot = lax.psum(jnp.sum(weighted * row_values, axis=1), 'tensor')]
    all_gather x2 -> x0, waiting for transfers between devices: 36.2 us -> none  [the longest x1 36.2 us: local(): lax.all_gather(recv_cots, 'dp', axis=0, tiled=True)]
    all_to_all x1 -> x0, blocking collectives: 29.9 us -> none  [local(): lax.all_to_all(send_cots, 'expert', split_axis=0, concat_axis=0, tiled=True)]
  transfers between devices with their start and end apart: 7 -> 0, of which waited for: 6 -> 0; matrix products, arithmetic and copies ran while one was open for 1% -> 0% of each run, Pallas kernels for 0% -> 0%
where the time goes in v1:
time: 142 us
  Pallas kernels  135 us (95%)
  local copies, waits for them, and re-layouts  3.31 us (2%)
  other arithmetic  2.69 us (2%)
    pallas_call x1, Pallas kernels, local(): pl.pallas_call(kernel, out_shape=jax.ShapeDtypeStruct((16, 384), F32), in...  135 us

profile of v1, /device:TPU:1, one launch (start us, length us, event | category | flops | bytes accessed | tf_op | source)
XLA Modules:
  0.0 142.0 jit_solution(6695545018087675335)
XLA Ops:
  0.0 0.0 copy-start
  0.7 0.1 copy-done
  0.8 0.1 constant_dynamic-slice_fusion
  0.8 0.1 copy.13
  1.6 0.7 multiply_bitcast_fusion
  2.3 0.7 convert_bitcast_fusion.1
  3.0 0.3 dynamic_update_slice.3.facts_ref
  3.3 0.0 copy-start.1
  3.3 0.8 dynamic_slice.7
  4.1 0.6 reshape.24.own_gain_ref
  4.7 1.3 convert_bitcast_fusion.gain_ref
  6.0 0.0 copy-done.1
  6.0 134.6 %moe_backward.1 = f32[16,384]{1,0:T(8,128)} custom-call(bf16[16,384]{1,0:T(8,128)(2,1)} %pool_ref.1, bf16[24,384]{1,0:T(8,128)(2,1)} %cot_ref.1, f32[8,768]{1,0:T(8,128)} %copy-done.1, f32[48,128]{1,0:T(8,128)} %convert_bitcast_fusion.gain_ref, f32[1,384]{1,0:T(1,128)} %reshape.24.own_gain_ref, bf16[48,128,128]{2,1,0:T(8,128)(2,1)} %bitcast.16, ...), custom_call_target="tpu_custom_call" | custom-call | tf_op jit(solution)/shard_map/moe_backward/pallas_call | solution.py:552
  140.6 1.3 copy.18
  (6 shorter events, 0.0 us)
Async XLA Ops:
  0.0 0.8 copy-start
  3.3 2.7 %copy-start.1 = (f32[8,768]{1,0:T(8,128)}, f32[8,768]{1,0:T(8,128)S(1)}, u32[]{:S(2)}) copy-start(f32[8,768]{1,0:T(8,128)S(1)} %dynamic_update_slice.3.facts_ref) | copy-start | bytes 73732

commit v2 on v1

--- a/solution.py
+++ b/solution.py
@@ -1,6 +1,3 @@
-import functools
-import heapq
-
 import jax
 import jax.numpy as jnp
 from jax import lax
@@ -29,7 +26,7 @@
         self.z = self.zh * 4 + self.zl
         self.send_sems, self.recv_sems = send_sems, recv_sems
         self.slots = {}
-        self.sent = []
+        self.sent = {}
 
     def device(self, x=None, y=None, z=None, c=None):
         x = self.x if x is None else x
@@ -40,6 +37,10 @@
 
     def copy(self, key, src, dst, device):
         slot = self.slots.setdefault(key, len(self.slots))
+        assert slot < Slots.STATIC
+        return self.copy_at(slot, src, dst, device)
+
+    def copy_at(self, slot, src, dst, device):
         return pltpu.make_async_remote_copy(
             src_ref=src,
             dst_ref=dst,
@@ -52,125 +53,272 @@
     def start(self, key, src, dst, device):
         copy = self.copy(key, src, dst, device)
         copy.start()
-        self.sent.append(copy)
+        self.sent[key] = copy
 
     def wait(self, key, dst):
         self.copy(key, dst, dst, self.device(c=1 - self.c)).wait_recv()
 
     def drain(self):
-        for copy in self.sent:
+        for copy in self.sent.values():
             copy.wait_send()
-        self.sent = []
+        self.sent = {}
+
+    def drain_sizes(self, sizes, stand_in):
+        for key, shape, dtype in sizes:
+            ref = stand_in(shape, dtype)
+            self.copy(key, ref, ref, self.device(c=1 - self.c)).wait_send()
 
 
 def kind(core, o):
     return "cot" if (core + o) % 2 == 0 else "pool"
 
 
-ORDERS = ("zyx", "xzy", "yxz")
-
-
-def region(net, o, done, axis=None, pos=None):
-    z = pos if axis == "z" else net.z
-    zh, zl = (KEEP, KEEP) if "z" in done else (z // 4, z % 4)
-    y = KEEP if "y" in done else (pos if axis == "y" else net.y)
-    x = KEEP if "x" in done else (pos if axis == "x" else net.x)
-    return (o, zh, y, x, zl)
-
-
-def gather_order(net, core, o, buf):
-    order = ORDERS[o]
-    now = 2.0
-    done = ""
-    for phase, axis in enumerate(order):
-        size = 16 if axis == "z" else 4
-        me = {"x": net.x, "y": net.y, "z": net.z}[axis]
-        last = phase == 2
-
-        def unit(pos, done=done, axis=axis):
-            return buf.at[region(net, o, done, axis, pos)]
-
-        def send(step, pos, key, unit=unit, axis=axis, size=size, me=me):
-            there = net.device(**{axis: (me + step) % size})
-            net.start((o, phase, key), unit(pos), unit(pos), there)
-
-        def to_partner(pos, name, unit=unit):
-            net.start((o, "partner", name), unit(pos), unit(pos), net.device(c=1 - net.c))
-
-        if last:
-            to_partner(me, 0)
-        if not last and axis != "z":
-            for step in (2, 1, 3):
-                send(step, me, step)
-            now += 3.0 if phase == 0 else 4.5
-            for step in (1, 3, 2):
-                yield now
-                net.wait((o, phase, step), unit((me - step) % size))
-        else:
-            right, left = (size // 2, size // 2 - 1) if core == 0 else (size // 2 - 1, size // 2)
-            if axis == "z":
-                tick = 3.4 if last else 2.2
-            else:
-                tick = 9.0
-            send(1, me, ("right", 1))
-            send(-1, me, ("left", 1))
-            for step in range(1, size // 2 + 1):
-                now += tick
-                for name, sign, count in (("right", 1, right), ("left", -1, left)):
-                    if step > count:
-                        continue
-                    yield now
-                    pos = (me - sign * step) % size
-                    net.wait((o, phase, (name, step)), unit(pos))
-                    if step < count:
-                        send(sign, pos, (name, step + 1))
-                    if last:
-                        to_partner(pos, sign * step)
-        done = done + axis
-
-
-def partner_names(core, o):
-    size = 16 if ORDERS[o][2] == "z" else 4
-    right, left = (size // 2, size // 2 - 1) if core == 0 else (size // 2 - 1, size // 2)
-    names = [0]
-    for step in range(1, size // 2 + 1):
-        names += [step] if step <= right else []
-        names += [-step] if step <= left else []
-    return names
+def spot(o, z, y, x):
+    zh, zl = (KEEP, KEEP) if z is None else (z // 4, z % 4)
+    return (o, zh, KEEP if y is None else y, KEEP if x is None else x, zl)
+
+
+def ring_steps(core, size):
+    return (size // 2, size // 2 - 1) if core == 0 else (size // 2 - 1, size // 2)
+
+
+class Slots:
+    STATIC = 110
+    LINE = STATIC
+    PLANE = LINE + 6 * 18
+    HAND = PLANE + 2 * 16 * 7
+    COUNT = HAND + 3 * 16
+
+    @staticmethod
+    def line(number, sign, step):
+        return Slots.LINE + number * 18 + (0 if sign == 1 else 9) + step
+
+    @staticmethod
+    def plane(o, distance, which):
+        return Slots.PLANE + (o * 16 + distance) * 7 + which
+
+    @staticmethod
+    def hand(o, distance):
+        return Slots.HAND + o * 16 + distance
+
+
+class Gather:
+    def __init__(self, net, core, bufs):
+        self.net, self.core, self.bufs = net, core, bufs
+        right, left = ring_steps(core, 16)
+        self.signs = ((1, 0, right), (-1, 1, left))
+        self.long = 1 if core == 0 else -1
+
+    def unit(self, o, z, y, x):
+        return self.bufs[kind(self.core, o)].at[spot(o, z, y, x)]
+
+    def send(self, slot, unit, device):
+        self.net.copy_at(slot, unit, unit, device).start()
+
+    def wait(self, slot, unit):
+        self.net.copy_at(slot, unit, unit, self.net.device(c=1 - self.net.c)).wait_recv()
+
+    def wait_sent(self, slot, unit):
+        self.net.copy_at(slot, unit, unit, self.net.device(c=1 - self.net.c)).wait_send()
+
+    def distance(self, sign, step):
+        return (16 - step) % 16 if sign == 1 else step % 16
+
+    def line_unit(self, number, pos):
+        net = self.net
+        if number < 2:
+            return self.unit(number, pos, net.y, net.x)
+        return self.unit(2, pos, None, (net.x - (number - 2)) % 4)
+
+    def line_send(self, number, sign, step):
+        net = self.net
+        unit = self.line_unit(number, (net.z + 16 - sign * (step - 1)) % 16)
+        self.send(Slots.line(number, sign, step), unit, net.device(z=(net.z + 16 + sign) % 16))
+
+    def line_step(self, number, sign, count, step):
+        unit = self.line_unit(number, (self.net.z + 16 - sign * step) % 16)
+        self.wait(Slots.line(number, sign, step), unit)
+
+        @pl.when(step < count)
+        def _():
+            self.line_send(number, sign, step + 1)
+
+    def one(self, o, z, step):
+        net = self.net
+        if o == 0:
+            return self.unit(o, z, (net.y + step) % 4, net.x)
+        return self.unit(o, z, net.y, (net.x + step) % 4)
+
+    def two(self, o, z, step):
+        net = self.net
+        if o == 0:
+            return self.unit(o, z, None, (net.x + step) % 4)
+        return self.unit(o, z, (net.y + step) % 4, None)
+
+    def along(self, o, ring, step):
+        net = self.net
+        if (o == 0) == (ring == 0):
+            return net.device(y=(net.y + step) % 4)
+        return net.device(x=(net.x + step) % 4)
+
+    def plane_start(self, o, sign, step):
+        d = self.distance(sign, step)
+        z = (self.net.z + d) % 16
+        for j in (2, 1, 3):
+            self.send(Slots.plane(o, d, j - 1), self.one(o, z, 0), self.along(o, 0, j))
+
+    def plane_turn(self, o, sign, step):
+        d = self.distance(sign, step)
+        z = (self.net.z + d) % 16
+        for j in (1, 3, 2):
+            self.wait(Slots.plane(o, d, j - 1), self.one(o, z, 4 - j))
+        for slot, way in ((3, self.long), (4, -self.long)):
+            self.send(Slots.plane(o, d, slot), self.two(o, z, 0), self.along(o, 1, 4 + way))
+
+    def plane_pass(self, o, sign, step):
+        d = self.distance(sign, step)
+        z = (self.net.z + d) % 16
+        self.wait(Slots.plane(o, d, 3), self.two(o, z, 4 - self.long))
+        self.send(
+            Slots.plane(o, d, 5), self.two(o, z, 4 - self.long), self.along(o, 1, 4 + self.long)
+        )
+        self.wait(Slots.plane(o, d, 4), self.two(o, z, 4 + self.long))
+
+    def plane_end(self, o, sign, step):
+        d = self.distance(sign, step)
+        z = (self.net.z + d) % 16
+        self.wait(Slots.plane(o, d, 5), self.two(o, z, 2))
+        self.hand_over(o, d)
+
+    def hand_over(self, o, d):
+        net = self.net
+        unit = self.unit(o, (net.z + d) % 16, None, None)
+        self.send(Slots.hand(o, d), unit, net.device(c=1 - net.c))
+
+    def begin(self):
+        net = self.net
+        for number in (0, 1):
+            self.line_send(number, 1, 1)
+            self.line_send(number, -1, 1)
+        own = self.unit(2, net.z, net.y, net.x)
+        for j in (2, 1, 3):
+            net.start(("y", j), own, own, net.device(y=(net.y + j) % 4))
+
+    def own_line(self):
+        net = self.net
+        for j in (1, 3, 2):
+            net.wait(("y", j), self.unit(2, net.z, (net.y + 4 - j) % 4, net.x))
+        self.line_send(2, 1, 1)
+        self.line_send(2, -1, 1)
+        own = self.unit(2, net.z, None, net.x)
+        for j in (2, 1, 3):
+            net.start(("x", j), own, own, net.device(x=(net.x + j) % 4))
+
+    def other_lines(self):
+        net = self.net
+        for j in (1, 3, 2):
+            net.wait(("x", j), self.unit(2, net.z, None, (net.x + 4 - j) % 4))
+            self.line_send(2 + j, 1, 1)
+            self.line_send(2 + j, -1, 1)
+        self.hand_over(2, 0)
+
+    def steps(self, s, facts):
+        for sign, first, count in self.signs:
+
+            @pl.when((s >= 1) & (s <= count))
+            def _():
+                self.line_step(0, sign, count, s)
+                self.line_step(1, sign, count, s)
+
+            @pl.when((s >= first) & (s <= count))
+            def _():
+                self.plane_start(0, sign, s)
+                self.plane_start(1, sign, s)
+
+        pl.when(s == 1)(self.own_line)
+        pl.when(s == 2)(self.other_lines)
+        for sign, first, count in self.signs:
+
+            @pl.when((s >= 3) & (s - 2 <= count))
+            def _():
+                for number in range(2, 6):
+                    self.line_step(number, sign, count, s - 2)
+                self.hand_over(2, self.distance(sign, s - 2))
+
+        for late, stage in ((1, self.plane_turn), (2, self.plane_pass), (3, self.plane_end)):
+            for sign, first, count in self.signs:
+
+                @pl.when((s >= late + first) & (s - late <= count))
+                def _():
+                    stage(0, sign, s - late)
+                    stage(1, sign, s - late)
+
+        for number, stage in enumerate(facts):
+            pl.when(s == 2 + 2 * number)(stage)
+
+    def run(self, facts):
+        def body(s, carry):
+            self.steps(s, facts)
+            return carry
+
+        self.begin()
+        lax.fori_loop(0, 12, body, 0)
+
+        def landed(d, carry):
+            for o in range(3):
+                other = self.bufs[kind(1 - self.core, o)]
+                self.wait(Slots.hand(o, d), other.at[spot(o, (self.net.z + d) % 16, None, None)])
+            return carry
+
+        lax.fori_loop(0, 16, landed, 0)
+
+    def drain(self):
+        def blocks(d, carry):
+            for o in (0, 1):
+                for which in range(3):
+                    self.wait_sent(Slots.plane(o, d, which), self.unit(o, 0, 0, 0))
+                for which in range(3, 6):
+                    self.wait_sent(Slots.plane(o, d, which), self.unit(o, 0, None, 0))
+            for o in range(3):
+                self.wait_sent(Slots.hand(o, d), self.unit(o, 0, None, None))
+            return carry
+
+        lax.fori_loop(0, 16, blocks, 0)
+        for sign, _, count in self.signs:
+
+            def lines(step, carry, sign=sign):
+                for number in range(6):
+                    unit = self.unit(min(number, 2), 0, 0 if number < 2 else None, 0)
+                    self.wait_sent(Slots.line(number, sign, step), unit)
+                return carry
+
+            lax.fori_loop(1, count + 1, lines, 0)
 
 
 def facts_stages(net, facts_ref, facts_got, facts_sum):
     net.start(("facts", 0), facts_ref, facts_got.at[0], net.device(c=1 - net.c))
-    yield 3.0
-    net.wait(("facts", 0), facts_got.at[0])
-    facts_sum[0] = facts_ref[...] + facts_got[0]
-    for j in (1, 2, 3):
-        there = net.device(z=net.zh * 4 + (net.zl + j) % 4)
-        net.start(("facts", j), facts_sum.at[0], facts_got.at[j], there)
-    yield 8.5
-    for j in (1, 2, 3):
-        net.wait(("facts", j), facts_got.at[j])
-    facts_sum[1] = facts_sum[0] + facts_got[1] + facts_got[2] + facts_got[3]
-    for j in (1, 2, 3):
-        there = net.device(x=(net.x + j) % 4)
-        net.start(("facts", 3 + j), facts_sum.at[1], facts_got.at[3 + j], there)
-    yield 14.5
-    for j in (1, 2, 3):
-        net.wait(("facts", 3 + j), facts_got.at[3 + j])
-    facts_sum[2] = facts_sum[1] + facts_got[4] + facts_got[5] + facts_got[6]
-
-
-def run_all(tasks):
-    heap = []
-    for number, task in enumerate(tasks):
-        time = next(task, None)
-        if time is not None:
-            heapq.heappush(heap, (time, number, task))
-    while heap:
-        _, number, task = heapq.heappop(heap)
-        time = next(task, None)
-        if time is not None:
-            heapq.heappush(heap, (time, number, task))
+
+    def pair():
+        net.wait(("facts", 0), facts_got.at[0])
+        facts_sum[0] = facts_ref[...] + facts_got[0]
+        for j in (1, 2, 3):
+            there = net.device(z=net.zh * 4 + (net.zl + j) % 4)
+            net.start(("facts", j), facts_sum.at[0], facts_got.at[j], there)
+
+    def near():
+        for j in (1, 2, 3):
+            net.wait(("facts", j), facts_got.at[j])
+        facts_sum[1] = facts_sum[0] + facts_got[1] + facts_got[2] + facts_got[3]
+        for j in (1, 2, 3):
+            there = net.device(x=(net.x + j) % 4)
+            net.start(("facts", 3 + j), facts_sum.at[1], facts_got.at[3 + j], there)
+
+    def whole():
+        for j in (1, 2, 3):
+            net.wait(("facts", 3 + j), facts_got.at[3 + j])
+        facts_sum[2] = facts_sum[1] + facts_got[4] + facts_got[5] + facts_got[6]
+
+    return pair, near, whole
 
 
 def gather(net, core, pool_ref, cot_ref, facts_ref, bufs, padded, landed, facts_got, facts_sum):
@@ -197,19 +345,9 @@
             other = landed[o].astype(F32)[:PROMPT]
             pair = [own, other] if core == 0 else [other, own]
             bufs["cot"][(o,) + here] = jnp.concatenate(pair, axis=0).astype(BF16)
-    run_all(
-        [gather_order(net, core, o, bufs[kind(core, o)]) for o in range(3)]
-        + [facts_stages(net, facts_ref, facts_got, facts_sum)]
-    )
-    for o in range(3):
-        axis = ORDERS[o][2]
-        size = 16 if axis == "z" else 4
-        me = {"x": net.x, "y": net.y, "z": net.z}[axis]
-        buf = bufs[kind(1 - core, o)]
-        for name in partner_names(1 - core, o):
-            unit = buf.at[region(net, o, ORDERS[o][:2], axis, (me - name) % size)]
-            net.wait((o, "partner", name), unit)
-    net.drain()
+    work = Gather(net, core, bufs)
+    work.run(facts_stages(net, facts_ref, facts_got, facts_sum))
+    return [(key, copy.src_ref.shape, copy.src_ref.dtype) for key, copy in net.sent.items()]
 
 
 def kernel(
@@ -217,7 +355,6 @@
     cot_ref,
     facts_ref,
     gain_ref,
-    own_gain_ref,
     w_gate_hbm,
     w_up_hbm,
     w_down_hbm,
@@ -252,10 +389,12 @@
     dot_x,
     dot_y,
     dot_z,
+    gain_all,
     weight_sems,
     send_sems,
     recv_sems,
 ):
+    gain_all[...] = gain_ref[...].astype(F32)
     net = Net(send_sems, recv_sems)
     partner = net.device(c=1 - net.c)
     loads = [
@@ -276,18 +415,39 @@
     pl.semaphore_wait(barrier, len(peers))
 
     bufs = {"pool": pool_buf, "cot": cot_buf}
+    sizes = [None, None]
     for core in range(2):
 
         @pl.when(net.c == core)
         def _():
             branch = Net(send_sems, recv_sems)
             branch.slots = net.slots
-            gather(
+            sizes[core] = gather(
                 branch, core, pool_ref, cot_ref, facts_ref, bufs, padded, landed, facts_got, facts_sum
             )
 
     for load in loads:
         load.wait()
+
+    def stand_in(shape, dtype):
+        if dtype == F32:
+            return facts_sum.at[0]
+        if shape == (16, 128):
+            return padded.at[0, pl.ds(0, 16)]
+        if shape == (32, 128):
+            return padded.at[0]
+        buf = pool_buf if shape[-2] == POOL_ROWS else cot_buf
+        ref = buf.at[(0,) * (7 - len(shape))]
+        assert ref.shape == shape
+        return ref
+
+    def drain_gather():
+        for core in range(2):
+
+            @pl.when(net.c == core)
+            def _():
+                net.drain_sizes(sizes[core], stand_in)
+                Gather(net, core, bufs).drain()
 
     hidden[...] = jnp.zeros_like(hidden)
     back[...] = jnp.zeros_like(back)
@@ -301,7 +461,7 @@
             for y in range(4):
                 value = pool_buf[o, zh, y].reshape(16 * POOL_ROWS, 128).astype(F32)
                 square = value * value if square is None else square + value * value
-                normed.append((value * gain_ref[pl.ds(blocks[y], 1), :]).astype(BF16))
+                normed.append((value * gain_all[pl.ds(blocks[y], 1), :]).astype(BF16))
             squares[...] += square
             weights = jnp.concatenate([w_in[b] for b in blocks], axis=0)
             hidden[...] += jnp.dot(
@@ -366,9 +526,11 @@
 
     net.start("dot_pair", dot_own, dot_pair, partner)
     spots = [(net.zh + step) % 4 for step in GROUP_ORDER]
-    for g, zh in enumerate(spots):
-
-        def other_step(y, carry, zh=zh):
+
+    def other(g):
+        zh = spots[g]
+
+        def other_step(y, carry):
             part_out[zh, y] = product(1 - net.c, zh, y).astype(BF16).reshape(4, 4, 16, 384)
             return carry
 
@@ -456,14 +618,18 @@
         for j in range(1, 16):
             net.start(("dot_z", j), dot_z.at[0], dot_z.at[j], net.device(z=(net.z + j) % 16))
 
+    other(0)
+    other(1)
     begin(0)
     dot_one()
+    other(2)
     begin(1)
+    dot_two()
     middle(0)
-    dot_two()
+    other(3)
     begin(2)
+    dot_three()
     middle(1)
-    dot_three()
     finish(0)
     begin(3)
     middle(2)
@@ -499,6 +665,8 @@
     scale = scales[pl.ds(pl.multiple_of(first, 16), 16), 0:1]
     factor = scale * scale * scale * own_dot / D
 
+    tile = (net.zh * 4 + net.y) * 3
+    own_gain = jnp.concatenate([gain_all[pl.ds(tile + o, 1), :] for o in range(3)], axis=1)
     total = plane[3, net.zl].astype(F32)
     for step in GROUP_ORDER:
         for j in range(4):
@@ -507,9 +675,10 @@
                 net.wait(("z", slot), last.at[slot])
                 total += last[slot].astype(F32)
     out_ref[...] = (
-        direct + scale * own_gain_ref[...] * total - pool_ref[...].astype(F32) * factor
+        direct + scale * own_gain * total - pool_ref[...].astype(F32) * factor
     )
     net.drain()
+    drain_gather()
 
 
 def local(
@@ -541,18 +710,15 @@
     facts = lax.dynamic_update_slice(
         jnp.zeros((8, TOKENS), F32), facts, (0, sequence * PROMPT)
     )
-    gain = norm_gain.astype(F32).reshape(48, 128)
-    own_gain = lax.dynamic_slice_in_dim(
-        norm_gain.astype(F32), lax.axis_index("tensor") * 384, 384, 0
-    ).reshape(1, 384)
+    gain = norm_gain.reshape(48, 128)
     vmem = pl.BlockSpec(memory_space=pltpu.VMEM)
     hbm = pl.BlockSpec(memory_space=pl.ANY)
     sums_shape = pltpu.VMEM((4, 4, 4, 4, 16, 384), BF16)
-    copies = 200
+    copies = Slots.COUNT
     return pl.pallas_call(
         kernel,
         out_shape=jax.ShapeDtypeStruct((16, 384), F32),
-        in_specs=[vmem] * 5 + [hbm] * 3,
+        in_specs=[vmem] * 4 + [hbm] * 3,
         out_specs=vmem,
         scratch_shapes=[
             pltpu.VMEM((3, 4, 4, 4, 4, POOL_ROWS, 128), BF16),
@@ -585,6 +751,7 @@
             pltpu.VMEM((4, 8, 128), F32),
             pltpu.VMEM((4, 8, 128), F32),
             pltpu.VMEM((16, 8, 128), F32),
+            pltpu.VMEM((48, 128), F32),
             pltpu.SemaphoreType.DMA((3,)),
             pltpu.SemaphoreType.DMA((copies,)),
             pltpu.SemaphoreType.DMA((copies,)),
@@ -598,7 +765,6 @@
         cotangent,
         facts,
         gain,
-        own_gain,
         w_gate.reshape(48, 128, 128),
         w_up.reshape(48, 128, 128),
         w_down[0],

time: 142 us -> 127 us (0.89)
  Pallas kernels: 135 us -> 121 us
    pallas_call x1, Pallas kernels: 135 us -> 121 us  [local(): pl.pallas_call(kernel, out_shape=jax.ShapeDtypeStruct((16, 384), F32), in...]
where the time goes in v2:
time: 127 us; the launch traced here: 126 us
  Pallas kernels  121 us (95%)
  local copies, waits for them, and re-layouts  2.46 us (2%)
  other arithmetic  1.38 us (1%)
  between operations  1.35 us (1%)
    pallas_call x1, Pallas kernels, local(): pl.pallas_call(kernel, out_shape=jax.ShapeDtypeStruct((16, 384), F32), in...  121 us

profile of v2, /device:TPU:1, one launch (start us, length us, event | category | flops | bytes accessed | tf_op | source)
XLA Modules:
  0.0 126.5 jit_solution(11423822985853478965)
XLA Ops:
  0.0 0.0 copy-start
  1.3 0.7 multiply_bitcast_fusion
  2.0 0.7 convert_bitcast_fusion
  2.7 0.0 copy-done
  2.7 0.1 constant_dynamic-slice_fusion
  2.8 0.1 copy.13
  2.9 0.3 dynamic_update_slice.3.facts_ref
  3.2 0.0 copy-start.1
  3.2 0.6 copy-done.1
  3.8 121.3 %moe_backward.1 = f32[16,384]{1,0:T(8,128)} custom-call(bf16[16,384]{1,0:T(8,128)(2,1)} %pool_ref.1, bf16[24,384]{1,0:T(8,128)(2,1)} %cot_ref.1, f32[8,768]{1,0:T(8,128)} %copy-done.1, bf16[48,128]{1,0:T(8,128)(2,1)} %bitcast.18, bf16[48,128,128]{2,1,0:T(8,128)(2,1)} %bitcast.15, bf16[48,128,128]{2,1,0:T(8,128)(2,1)} %bitcast.16, bf16[128,6144]{1,0:T(8,128)(2,1)} %bitcast.17), custom_call_target="tpu_custom_call" | custom-call | tf_op jit(solution)/shard_map/moe_backward/pallas_call | solution.py:718
  125.1 1.3 %copy.18 = f32[16,384]{1,0:T(8,128)} copy(f32[16,384]{1,0:T(8,128)} %moe_backward.1) | data formatting | bytes 49152
  (6 shorter events, 0.0 us)
Async XLA Ops:
  0.0 2.7 %copy-start = (s32[256,24]{0,1:T(8,128)S(1)}, s32[256,24]{0,1:T(8,128)}, u32[]{:S(2)}) copy-start(s32[256,24]{0,1:T(8,128)} %param.12) | copy-start | bytes 73732
  3.2 0.6 copy-start.1

commit v3 on v2

--- a/solution.py
+++ b/solution.py
@@ -14,6 +14,8 @@
 GROUP_ORDER = (2, 1, 3, 0)
 NT = (((1,), (1,)), ((), ()))
 KEEP = slice(None)
+NEAR = (1, 15)
+TURN, PASS, END, ROUND = 1, 2, 3, 4
 
 
 class Net:
@@ -83,11 +85,12 @@
 
 
 class Slots:
-    STATIC = 110
+    STATIC = 140
     LINE = STATIC
     PLANE = LINE + 6 * 18
     HAND = PLANE + 2 * 16 * 7
-    COUNT = HAND + 3 * 16
+    Z = HAND + 3 * 16
+    COUNT = Z + 16
 
     @staticmethod
     def line(number, sign, step):
@@ -239,13 +242,13 @@
         pl.when(s == 2)(self.other_lines)
         for sign, first, count in self.signs:
 
-            @pl.when((s >= 3) & (s - 2 <= count))
+            @pl.when((s >= ROUND + 1) & (s - ROUND <= count))
             def _():
                 for number in range(2, 6):
-                    self.line_step(number, sign, count, s - 2)
-                self.hand_over(2, self.distance(sign, s - 2))
-
-        for late, stage in ((1, self.plane_turn), (2, self.plane_pass), (3, self.plane_end)):
+                    self.line_step(number, sign, count, s - ROUND)
+                self.hand_over(2, self.distance(sign, s - ROUND))
+
+        for late, stage in ((TURN, self.plane_turn), (PASS, self.plane_pass), (END, self.plane_end)):
             for sign, first, count in self.signs:
 
                 @pl.when((s >= late + first) & (s - late <= count))
@@ -262,15 +265,16 @@
             return carry
 
         self.begin()
-        lax.fori_loop(0, 12, body, 0)
-
-        def landed(d, carry):
-            for o in range(3):
-                other = self.bufs[kind(1 - self.core, o)]
-                self.wait(Slots.hand(o, d), other.at[spot(o, (self.net.z + d) % 16, None, None)])
+        lax.fori_loop(0, max(END, ROUND) + 9, body, 0)
+
+    def landed(self, o):
+        other = self.bufs[kind(1 - self.core, o)]
+
+        def body(d, carry):
+            self.wait(Slots.hand(o, d), other.at[spot(o, (self.net.z + d) % 16, None, None)])
             return carry
 
-        lax.fori_loop(0, 16, landed, 0)
+        lax.fori_loop(0, 16, body, 0)
 
     def drain(self):
         def blocks(d, carry):
@@ -350,10 +354,35 @@
     return [(key, copy.src_ref.shape, copy.src_ref.dtype) for key, copy in net.sent.items()]
 
 
+def build_facts(net, ids_ref, tenant_ref, lengths_ref, routes_ref, route_weight_ref, facts_ref):
+    sequence = (net.x * 4 + net.zl) * 2 + net.c
+    row = lax.broadcasted_iota(jnp.int32, (PROMPT, TOKENS), 0) + sequence * PROMPT
+    place = jnp.where(lax.broadcasted_iota(jnp.int32, (PROMPT, TOKENS), 1) == row, 1.0, 0.0)
+    ids = jnp.broadcast_to(ids_ref[pl.ds(tenant_ref[0], 1), :].astype(F32), (8, PROMPT))
+    spread = jnp.dot(
+        ids, place, precision=lax.Precision.HIGHEST, preferred_element_type=F32
+    )
+    facts_ref[...] = jnp.zeros_like(facts_ref)
+    facts_ref[0:1] = spread[0:1]
+    live = place * jnp.where(
+        lax.broadcasted_iota(jnp.int32, (PROMPT, TOKENS), 0) < lengths_ref[0], 1.0, 0.0
+    )
+    facts_ref[1:2] = jnp.sum(live, axis=0, keepdims=True)
+    for k in range(2):
+        route = routes_ref[:, k : k + 1].astype(F32)
+        facts_ref[2 + k : 3 + k] = jnp.sum(place * route, axis=0, keepdims=True)
+        weight = route_weight_ref[:, k : k + 1]
+        facts_ref[4 + k : 5 + k] = jnp.sum(live * weight, axis=0, keepdims=True)
+
+
 def kernel(
     pool_ref,
     cot_ref,
-    facts_ref,
+    ids_ref,
+    tenant_ref,
+    lengths_ref,
+    routes_ref,
+    route_weight_ref,
     gain_ref,
     w_gate_hbm,
     w_up_hbm,
@@ -390,6 +419,7 @@
     dot_y,
     dot_z,
     gain_all,
+    facts_ref,
     weight_sems,
     send_sems,
     recv_sems,
@@ -405,11 +435,12 @@
     for load in loads:
         load.start()
 
+    build_facts(net, ids_ref, tenant_ref, lengths_ref, routes_ref, route_weight_ref, facts_ref)
     barrier = pltpu.get_barrier_semaphore()
     peers = [partner]
     for j in (1, 2, 3):
         peers += [net.device(x=(net.x + j) % 4), net.device(y=(net.y + j) % 4)]
-    peers += [net.device(z=(net.z + j) % 16) for j in range(1, 16)]
+    peers += [net.device(z=(net.z + j) % 16) for j in NEAR]
     for peer in peers:
         pl.semaphore_signal(barrier, inc=1, device_id=peer, device_id_type=MESH)
     pl.semaphore_wait(barrier, len(peers))
@@ -475,6 +506,12 @@
             )
             back[...] += lax.dot_general(cots, downs, NT, preferred_element_type=F32)
             return carry
+
+        for core in range(2):
+
+            @pl.when(net.c == core)
+            def _():
+                Gather(net, core, bufs).landed(o)
 
         lax.fori_loop(0, 4, columns_step, 0)
 
@@ -549,52 +586,52 @@
             return carry
 
         lax.fori_loop(0, 4, own_step, 0)
+        for h in range(2):
+            for j in (2, 1, 3):
+                x, y = (net.x + j) % 4, (net.y + j) % 4
+                to_x, to_y = net.device(x=x), net.device(y=y)
+                net.start(("a1", g, h, j), sums.at[zh, :, x, h], first_a.at[g, h, j - 1], to_x)
+                net.start(("b1", g, h, j), sums.at[zh, y, :, 2 + h], first_b.at[g, h, j - 1], to_y)
+
+    def middle(g, h):
+        zh = spots[g]
+        for j in (1, 2, 3):
+            net.wait(("a1", g, h, j), first_a.at[g, h, j - 1])
+            net.wait(("b1", g, h, j), first_b.at[g, h, j - 1])
+        own_a = sums[zh, :, net.x, h].astype(F32)
+        own_b = sums[zh, net.y, :, 2 + h].astype(F32)
+        for j in range(3):
+            own_a += first_a[g, h, j].astype(F32)
+            own_b += first_b[g, h, j].astype(F32)
+        mid_a[g, h] = own_a.astype(BF16)
+        mid_b[g, h] = own_b.astype(BF16)
         for j in (2, 1, 3):
             x, y = (net.x + j) % 4, (net.y + j) % 4
-            net.start(
-                ("a1", g, j), sums.at[zh, :, x, pl.ds(0, 2)], first_a.at[g, j - 1], net.device(x=x)
-            )
-            net.start(
-                ("b1", g, j), sums.at[zh, y, :, pl.ds(2, 2)], first_b.at[g, j - 1], net.device(y=y)
-            )
-
-    def middle(g):
-        zh = spots[g]
-        for j in (1, 2, 3):
-            net.wait(("a1", g, j), first_a.at[g, j - 1])
-            net.wait(("b1", g, j), first_b.at[g, j - 1])
-        own_a = sums[zh, :, net.x, 0:2].astype(F32)
-        own_b = sums[zh, net.y, :, 2:4].astype(F32)
+            to_x, to_y = net.device(x=x), net.device(y=y)
+            net.start(("a2", g, h, j), mid_a.at[g, h, y], second_a.at[g, h, j - 1], to_y)
+            net.start(("b2", g, h, j), mid_b.at[g, h, x], second_b.at[g, h, j - 1], to_x)
+
+    def line_copy(g, zl):
+        slot = GROUP_ORDER[g] * 4 + (zl + 4 - net.zl) % 4
+        there = net.device(z=spots[g] * 4 + zl)
+        return net.copy_at(Slots.Z + slot, plane.at[g, zl], last.at[slot], there)
+
+    def finish(g, h):
+        for j in (1, 2, 3):
+            net.wait(("a2", g, h, j), second_a.at[g, h, j - 1])
+            net.wait(("b2", g, h, j), second_b.at[g, h, j - 1])
+        own_a = mid_a[g, h, net.y].astype(F32)
+        own_b = mid_b[g, h, net.x].astype(F32)
         for j in range(3):
-            own_a += first_a[g, j].astype(F32)
-            own_b += first_b[g, j].astype(F32)
-        mid_a[g] = own_a.astype(BF16)
-        mid_b[g] = own_b.astype(BF16)
-        for j in (2, 1, 3):
-            x, y = (net.x + j) % 4, (net.y + j) % 4
-            net.start(("a2", g, j), mid_a.at[g, y], second_a.at[g, j - 1], net.device(y=y))
-            net.start(("b2", g, j), mid_b.at[g, x], second_b.at[g, j - 1], net.device(x=x))
-
-    def finish(g):
-        step = GROUP_ORDER[g]
-        for j in (1, 2, 3):
-            net.wait(("a2", g, j), second_a.at[g, j - 1])
-            net.wait(("b2", g, j), second_b.at[g, j - 1])
-        own_a = mid_a[g, net.y].astype(F32)
-        own_b = mid_b[g, net.x].astype(F32)
-        for j in range(3):
-            own_a += second_a[g, j].astype(F32)
-            own_b += second_b[g, j].astype(F32)
-        plane[g, 0:2] = own_a.astype(BF16)
-        plane[g, 2:4] = own_b.astype(BF16)
-        for j in range(4):
-            if step == 0 and j == 0:
-                continue
-            zl = (net.zl + j) % 4
-            slot = step * 4 + j
-            net.start(
-                ("z", slot), plane.at[g, zl], last.at[slot], net.device(z=spots[g] * 4 + zl)
-            )
+            own_a += second_a[g, h, j].astype(F32)
+            own_b += second_b[g, h, j].astype(F32)
+        plane[g, h] = own_a.astype(BF16)
+        plane[g, 2 + h] = own_b.astype(BF16)
+        for zl in (h, 2 + h):
+            if GROUP_ORDER[g] > 0:
+                line_copy(g, zl).start()
+            else:
+                pl.when(net.zl != zl)(lambda zl=zl: line_copy(g, zl).start())
 
     def dot_one():
         net.wait("dot_pair", dot_pair)
@@ -625,15 +662,21 @@
     other(2)
     begin(1)
     dot_two()
-    middle(0)
+    middle(0, 0)
+    middle(0, 1)
     other(3)
     begin(2)
     dot_three()
-    middle(1)
-    finish(0)
+    middle(1, 0)
+    finish(0, 0)
+    middle(1, 1)
+    finish(0, 1)
     begin(3)
-    middle(2)
-    finish(1)
+    drain_gather()
+    middle(2, 0)
+    finish(1, 0)
+    middle(2, 1)
+    finish(1, 1)
 
     first = ((net.x * 4 + net.zl) * 2 + net.c) * 16
     own_number = (lax.broadcasted_iota(jnp.int32, (16, 1), 0) + first).astype(F32)
@@ -650,9 +693,13 @@
         axis=1,
     )
 
-    middle(3)
-    finish(2)
-    finish(3)
+    middle(3, 0)
+    finish(2, 0)
+    middle(3, 1)
+    finish(2, 1)
+    finish(3, 0)
+    finish(3, 1)
+    net.drain()
 
     for j in range(1, 16):
         net.wait(("dot_z", j), dot_z.at[j])
@@ -672,13 +719,14 @@
         for j in range(4):
             slot = step * 4 + j
             if slot > 0:
-                net.wait(("z", slot), last.at[slot])
+                arrival = last.at[slot]
+                net.copy_at(Slots.Z + slot, arrival, arrival, partner).wait_recv()
                 total += last[slot].astype(F32)
     out_ref[...] = (
         direct + scale * own_gain * total - pool_ref[...].astype(F32) * factor
     )
-    net.drain()
-    drain_gather()
+    for slot in range(1, 16):
+        net.copy_at(Slots.Z + slot, plane.at[0, 0], last.at[slot], partner).wait_send()
 
 
 def local(
@@ -694,31 +742,16 @@
     w_up,
     w_down,
 ):
-    sequence = lax.axis_index(("dp", "expert"))
-    ids = prompt_ids[tenant[0]]
-    live = (jnp.arange(PROMPT, dtype=jnp.int32) < lengths[0]).astype(F32)
-    facts = jnp.concatenate(
-        [
-            ids[None].astype(F32),
-            live[None],
-            routes.T.astype(F32),
-            route_weight.T * live[None],
-            jnp.zeros((2, PROMPT), F32),
-        ],
-        axis=0,
-    )
-    facts = lax.dynamic_update_slice(
-        jnp.zeros((8, TOKENS), F32), facts, (0, sequence * PROMPT)
-    )
     gain = norm_gain.reshape(48, 128)
     vmem = pl.BlockSpec(memory_space=pltpu.VMEM)
     hbm = pl.BlockSpec(memory_space=pl.ANY)
+    smem = pl.BlockSpec(memory_space=pltpu.SMEM)
     sums_shape = pltpu.VMEM((4, 4, 4, 4, 16, 384), BF16)
     copies = Slots.COUNT
     return pl.pallas_call(
         kernel,
         out_shape=jax.ShapeDtypeStruct((16, 384), F32),
-        in_specs=[vmem] * 4 + [hbm] * 3,
+        in_specs=[vmem] * 3 + [smem] * 2 + [vmem] * 3 + [hbm] * 3,
         out_specs=vmem,
         scratch_shapes=[
             pltpu.VMEM((3, 4, 4, 4, 4, POOL_ROWS, 128), BF16),
@@ -737,12 +770,12 @@
             sums_shape,
             sums_shape,
             sums_shape,
-            pltpu.VMEM((4, 3, 4, 2, 16, 384), BF16),
-            pltpu.VMEM((4, 3, 4, 2, 16, 384), BF16),
-            pltpu.VMEM((4, 4, 2, 16, 384), BF16),
-            pltpu.VMEM((4, 4, 2, 16, 384), BF16),
-            pltpu.VMEM((4, 3, 2, 16, 384), BF16),
-            pltpu.VMEM((4, 3, 2, 16, 384), BF16),
+            pltpu.VMEM((4, 2, 3, 4, 16, 384), BF16),
+            pltpu.VMEM((4, 2, 3, 4, 16, 384), BF16),
+            pltpu.VMEM((4, 2, 4, 16, 384), BF16),
+            pltpu.VMEM((4, 2, 4, 16, 384), BF16),
+            pltpu.VMEM((4, 2, 3, 16, 384), BF16),
+            pltpu.VMEM((4, 2, 3, 16, 384), BF16),
             pltpu.VMEM((4, 4, 16, 384), BF16),
             pltpu.VMEM((16, 16, 384), BF16),
             pltpu.VMEM((8, 512), F32),
@@ -752,6 +785,7 @@
             pltpu.VMEM((4, 8, 128), F32),
             pltpu.VMEM((16, 8, 128), F32),
             pltpu.VMEM((48, 128), F32),
+            pltpu.VMEM((8, TOKENS), F32),
             pltpu.SemaphoreType.DMA((3,)),
             pltpu.SemaphoreType.DMA((copies,)),
             pltpu.SemaphoreType.DMA((copies,)),
@@ -763,7 +797,11 @@
     )(
         pool,
         cotangent,
-        facts,
+        prompt_ids,
+        tenant,
+        lengths,
+        routes,
+        route_weight,
         gain,
         w_gate.reshape(48, 128, 128),
         w_up.reshape(48, 128, 128),

time: 127 us -> 124 us (0.976)
  Pallas kernels: 121 us -> 117 us
  local copies, waits for them, and re-layouts: 2.46 us -> 5.53 us
  other arithmetic: 1.38 us -> 0 us
    pallas_call x1, Pallas kernels: 121 us -> 117 us  [local(): pl.pallas_call(kernel, out_shape=jax.ShapeDtypeStruct((16, 384), F32), in...]
    unnamed x6 -> x4, local copies, waits for them, and re-layouts: 2.04 us -> 5.53 us
where the time goes in v3:
time: 124 us
  Pallas kernels  117 us (94%)
  local copies, waits for them, and re-layouts  5.53 us (4%)
  between operations  1.31 us (1%)
    pallas_call x1, Pallas kernels, local(): pl.pallas_call(kernel, out_shape=jax.ShapeDtypeStruct((16, 384), F32), in...  117 us
    unnamed x4, local copies, waits for them, and re-layouts  5.53 us

profile of v3, /device:TPU:1, one launch (start us, length us, event | category | flops | bytes accessed | tf_op | source)
XLA Modules:
  0.0 124.1 jit_solution(2647529518099060459)
XLA Ops:
  1.3 1.4 %copy.13.routes_ref = s32[24,2]{1,0:T(8,128)} copy(s32[24,2]{0,1:T(2,128)} %param.15) | data formatting | bytes 384 | tf_op args[4]
  2.7 1.4 %copy.14.route_weight_ref = f32[24,2]{1,0:T(8,128)} copy(f32[24,2]{0,1:T(2,128)} %param.16) | data formatting | bytes 384 | tf_op args[5]
  4.0 1.5 %copy.12.ids_ref = s32[256,24]{1,0:T(8,128)} copy(s32[256,24]{0,1:T(8,128)} %param.12) | data formatting | bytes 49152 | tf_op args[1]
  5.5 117.2 %moe_backward.1 = f32[16,384]{1,0:T(8,128)} custom-call(bf16[16,384]{1,0:T(8,128)(2,1)} %pool_ref.1, bf16[24,384]{1,0:T(8,128)(2,1)} %cot_ref.1, s32[256,24]{1,0:T(8,128)} %copy.12.ids_ref, s32[1]{0:T(128)S(6)} %copy.16.tenant_ref, s32[1]{0:T(128)S(6)} %copy.17.lengths_ref, s32[24,2]{1,0:T(8,128)} %copy.13.routes_ref, f32[24,2]{1,0:T(8,128)} %copy.14.route_weight_ref, ...), custom_call_target="tpu_custom_call" | custom-call | tf_op jit(solution)/shard_map/moe_backward/pallas_call | solution.py:751
  122.7 1.3 %copy.18 = f32[16,384]{1,0:T(8,128)} copy(f32[16,384]{1,0:T(8,128)} %moe_backward.1) | data formatting | bytes 49152

commit v4 on v3

--- a/solution.py
+++ b/solution.py
@@ -18,13 +18,21 @@
 TURN, PASS, END, ROUND = 1, 2, 3, 4
 
 
+def mod(value, size):
+    return value % size if isinstance(value, int) else lax.rem(value, size)
+
+
+def div(value, size):
+    return value // size if isinstance(value, int) else lax.div(value, size)
+
+
 class Net:
     def __init__(self, send_sems, recv_sems):
         self.x = lax.axis_index("dp")
         expert = lax.axis_index("expert")
         tensor = lax.axis_index("tensor")
-        self.zl, self.c = expert // 2, expert % 2
-        self.zh, self.y = tensor // 4, tensor % 4
+        self.zl, self.c = div(expert, 2), mod(expert, 2)
+        self.zh, self.y = div(tensor, 4), mod(tensor, 4)
         self.z = self.zh * 4 + self.zl
         self.send_sems, self.recv_sems = send_sems, recv_sems
         self.slots = {}
@@ -35,7 +43,7 @@
         y = self.y if y is None else y
         z = self.z if z is None else z
         c = self.c if c is None else c
-        return (x, (z % 4) * 2 + c, (z // 4) * 4 + y)
+        return (x, (mod(z, 4)) * 2 + c, (div(z, 4)) * 4 + y)
 
     def copy(self, key, src, dst, device):
         slot = self.slots.setdefault(key, len(self.slots))
@@ -72,16 +80,16 @@
 
 
 def kind(core, o):
-    return "cot" if (core + o) % 2 == 0 else "pool"
+    return "cot" if mod(core + o, 2) == 0 else "pool"
 
 
 def spot(o, z, y, x):
-    zh, zl = (KEEP, KEEP) if z is None else (z // 4, z % 4)
+    zh, zl = (KEEP, KEEP) if z is None else (div(z, 4), mod(z, 4))
     return (o, zh, KEEP if y is None else y, KEEP if x is None else x, zl)
 
 
 def ring_steps(core, size):
-    return (size // 2, size // 2 - 1) if core == 0 else (size // 2 - 1, size // 2)
+    return (div(size, 2), div(size, 2) - 1) if core == 0 else (div(size, 2) - 1, div(size, 2))
 
 
 class Slots:
@@ -125,21 +133,21 @@
         self.net.copy_at(slot, unit, unit, self.net.device(c=1 - self.net.c)).wait_send()
 
     def distance(self, sign, step):
-        return (16 - step) % 16 if sign == 1 else step % 16
+        return mod(16 - step, 16) if sign == 1 else mod(step, 16)
 
     def line_unit(self, number, pos):
         net = self.net
         if number < 2:
             return self.unit(number, pos, net.y, net.x)
-        return self.unit(2, pos, None, (net.x - (number - 2)) % 4)
+        return self.unit(2, pos, None, mod(net.x + 6 - number, 4))
 
     def line_send(self, number, sign, step):
         net = self.net
-        unit = self.line_unit(number, (net.z + 16 - sign * (step - 1)) % 16)
-        self.send(Slots.line(number, sign, step), unit, net.device(z=(net.z + 16 + sign) % 16))
+        unit = self.line_unit(number, mod(net.z + 16 - sign * (step - 1), 16))
+        self.send(Slots.line(number, sign, step), unit, net.device(z=mod(net.z + 16 + sign, 16)))
 
     def line_step(self, number, sign, count, step):
-        unit = self.line_unit(number, (self.net.z + 16 - sign * step) % 16)
+        unit = self.line_unit(number, mod(self.net.z + 16 - sign * step, 16))
         self.wait(Slots.line(number, sign, step), unit)
 
         @pl.when(step < count)
@@ -149,30 +157,30 @@
     def one(self, o, z, step):
         net = self.net
         if o == 0:
-            return self.unit(o, z, (net.y + step) % 4, net.x)
-        return self.unit(o, z, net.y, (net.x + step) % 4)
+            return self.unit(o, z, mod(net.y + step, 4), net.x)
+        return self.unit(o, z, net.y, mod(net.x + step, 4))
 
     def two(self, o, z, step):
         net = self.net
         if o == 0:
-            return self.unit(o, z, None, (net.x + step) % 4)
-        return self.unit(o, z, (net.y + step) % 4, None)
+            return self.unit(o, z, None, mod(net.x + step, 4))
+        return self.unit(o, z, mod(net.y + step, 4), None)
 
     def along(self, o, ring, step):
         net = self.net
         if (o == 0) == (ring == 0):
-            return net.device(y=(net.y + step) % 4)
-        return net.device(x=(net.x + step) % 4)
+            return net.device(y=mod(net.y + step, 4))
+        return net.device(x=mod(net.x + step, 4))
 
     def plane_start(self, o, sign, step):
         d = self.distance(sign, step)
-        z = (self.net.z + d) % 16
+        z = mod(self.net.z + d, 16)
         for j in (2, 1, 3):
             self.send(Slots.plane(o, d, j - 1), self.one(o, z, 0), self.along(o, 0, j))
 
     def plane_turn(self, o, sign, step):
         d = self.distance(sign, step)
-        z = (self.net.z + d) % 16
+        z = mod(self.net.z + d, 16)
         for j in (1, 3, 2):
             self.wait(Slots.plane(o, d, j - 1), self.one(o, z, 4 - j))
         for slot, way in ((3, self.long), (4, -self.long)):
@@ -180,7 +188,7 @@
 
     def plane_pass(self, o, sign, step):
         d = self.distance(sign, step)
-        z = (self.net.z + d) % 16
+        z = mod(self.net.z + d, 16)
         self.wait(Slots.plane(o, d, 3), self.two(o, z, 4 - self.long))
         self.send(
             Slots.plane(o, d, 5), self.two(o, z, 4 - self.long), self.along(o, 1, 4 + self.long)
@@ -189,13 +197,13 @@
 
     def plane_end(self, o, sign, step):
         d = self.distance(sign, step)
-        z = (self.net.z + d) % 16
+        z = mod(self.net.z + d, 16)
         self.wait(Slots.plane(o, d, 5), self.two(o, z, 2))
         self.hand_over(o, d)
 
     def hand_over(self, o, d):
         net = self.net
-        unit = self.unit(o, (net.z + d) % 16, None, None)
+        unit = self.unit(o, mod(net.z + d, 16), None, None)
         self.send(Slots.hand(o, d), unit, net.device(c=1 - net.c))
 
     def begin(self):
@@ -205,22 +213,22 @@
             self.line_send(number, -1, 1)
         own = self.unit(2, net.z, net.y, net.x)
         for j in (2, 1, 3):
-            net.start(("y", j), own, own, net.device(y=(net.y + j) % 4))
+            net.start(("y", j), own, own, net.device(y=mod(net.y + j, 4)))
 
     def own_line(self):
         net = self.net
         for j in (1, 3, 2):
-            net.wait(("y", j), self.unit(2, net.z, (net.y + 4 - j) % 4, net.x))
+            net.wait(("y", j), self.unit(2, net.z, mod(net.y + 4 - j, 4), net.x))
         self.line_send(2, 1, 1)
         self.line_send(2, -1, 1)
         own = self.unit(2, net.z, None, net.x)
         for j in (2, 1, 3):
-            net.start(("x", j), own, own, net.device(x=(net.x + j) % 4))
+            net.start(("x", j), own, own, net.device(x=mod(net.x + j, 4)))
 
     def other_lines(self):
         net = self.net
         for j in (1, 3, 2):
-            net.wait(("x", j), self.unit(2, net.z, None, (net.x + 4 - j) % 4))
+            net.wait(("x", j), self.unit(2, net.z, None, mod(net.x + 4 - j, 4)))
             self.line_send(2 + j, 1, 1)
             self.line_send(2 + j, -1, 1)
         self.hand_over(2, 0)
@@ -271,7 +279,7 @@
         other = self.bufs[kind(1 - self.core, o)]
 
         def body(d, carry):
-            self.wait(Slots.hand(o, d), other.at[spot(o, (self.net.z + d) % 16, None, None)])
+            self.wait(Slots.hand(o, d), other.at[spot(o, mod(self.net.z + d, 16), None, None)])
             return carry
 
         lax.fori_loop(0, 16, body, 0)
@@ -306,7 +314,7 @@
         net.wait(("facts", 0), facts_got.at[0])
         facts_sum[0] = facts_ref[...] + facts_got[0]
         for j in (1, 2, 3):
-            there = net.device(z=net.zh * 4 + (net.zl + j) % 4)
+            there = net.device(z=net.zh * 4 + mod(net.zl + j, 4))
             net.start(("facts", j), facts_sum.at[0], facts_got.at[j], there)
 
     def near():
@@ -314,7 +322,7 @@
             net.wait(("facts", j), facts_got.at[j])
         facts_sum[1] = facts_sum[0] + facts_got[1] + facts_got[2] + facts_got[3]
         for j in (1, 2, 3):
-            there = net.device(x=(net.x + j) % 4)
+            there = net.device(x=mod(net.x + j, 4))
             net.start(("facts", 3 + j), facts_sum.at[1], facts_got.at[3 + j], there)
 
     def whole():
@@ -439,8 +447,8 @@
     barrier = pltpu.get_barrier_semaphore()
     peers = [partner]
     for j in (1, 2, 3):
-        peers += [net.device(x=(net.x + j) % 4), net.device(y=(net.y + j) % 4)]
-    peers += [net.device(z=(net.z + j) % 16) for j in NEAR]
+        peers += [net.device(x=mod(net.x + j, 4)), net.device(y=mod(net.y + j, 4))]
+    peers += [net.device(z=mod(net.z + j, 16)) for j in NEAR]
     for peer in peers:
         pl.semaphore_signal(barrier, inc=1, device_id=peer, device_id_type=MESH)
     pl.semaphore_wait(barrier, len(peers))
@@ -562,7 +570,7 @@
         return lax.dot_general(grads[parity], weights, NT, preferred_element_type=F32)
 
     net.start("dot_pair", dot_own, dot_pair, partner)
-    spots = [(net.zh + step) % 4 for step in GROUP_ORDER]
+    spots = [mod(net.zh + step, 4) for step in GROUP_ORDER]
 
     def other(g):
         zh = spots[g]
@@ -574,7 +582,7 @@
         lax.fori_loop(0, 4, other_step, 0)
         net.start(("part", g), part_out.at[zh], part_in.at[zh], partner)
 
-    lanes = [pl.ds(pl.multiple_of((net.x + j) % 4 * 128, 128), 128) for j in range(4)]
+    lanes = [pl.ds(pl.multiple_of(mod(net.x + j, 4) * 128, 128), 128) for j in range(4)]
 
     def begin(g):
         zh = spots[g]
@@ -588,7 +596,7 @@
         lax.fori_loop(0, 4, own_step, 0)
         for h in range(2):
             for j in (2, 1, 3):
-                x, y = (net.x + j) % 4, (net.y + j) % 4
+                x, y = mod(net.x + j, 4), mod(net.y + j, 4)
                 to_x, to_y = net.device(x=x), net.device(y=y)
                 net.start(("a1", g, h, j), sums.at[zh, :, x, h], first_a.at[g, h, j - 1], to_x)
                 net.start(("b1", g, h, j), sums.at[zh, y, :, 2 + h], first_b.at[g, h, j - 1], to_y)
@@ -606,13 +614,13 @@
         mid_a[g, h] = own_a.astype(BF16)
         mid_b[g, h] = own_b.astype(BF16)
         for j in (2, 1, 3):
-            x, y = (net.x + j) % 4, (net.y + j) % 4
+            x, y = mod(net.x + j, 4), mod(net.y + j, 4)
             to_x, to_y = net.device(x=x), net.device(y=y)
             net.start(("a2", g, h, j), mid_a.at[g, h, y], second_a.at[g, h, j - 1], to_y)
             net.start(("b2", g, h, j), mid_b.at[g, h, x], second_b.at[g, h, j - 1], to_x)
 
     def line_copy(g, zl):
-        slot = GROUP_ORDER[g] * 4 + (zl + 4 - net.zl) % 4
+        slot = GROUP_ORDER[g] * 4 + mod(zl + 4 - net.zl, 4)
         there = net.device(z=spots[g] * 4 + zl)
         return net.copy_at(Slots.Z + slot, plane.at[g, zl], last.at[slot], there)
 
@@ -638,7 +646,7 @@
         dot_sum[...] = dot_own[...] + dot_pair[...]
         for j in (1, 2, 3):
             net.start(
-                ("dot_x", j), dot_sum.at[:, lanes[j]], dot_x.at[j], net.device(x=(net.x + j) % 4)
+                ("dot_x", j), dot_sum.at[:, lanes[j]], dot_x.at[j], net.device(x=mod(net.x + j, 4))
             )
 
     def dot_two():
@@ -646,14 +654,14 @@
             net.wait(("dot_x", j), dot_x.at[j])
         dot_y[0] = dot_sum[:, lanes[0]] + dot_x[1] + dot_x[2] + dot_x[3]
         for j in (1, 2, 3):
-            net.start(("dot_y", j), dot_y.at[0], dot_y.at[j], net.device(y=(net.y + j) % 4))
+            net.start(("dot_y", j), dot_y.at[0], dot_y.at[j], net.device(y=mod(net.y + j, 4)))
 
     def dot_three():
         for j in (1, 2, 3):
             net.wait(("dot_y", j), dot_y.at[j])
         dot_z[0] = dot_y[0] + dot_y[1] + dot_y[2] + dot_y[3]
         for j in range(1, 16):
-            net.start(("dot_z", j), dot_z.at[0], dot_z.at[j], net.device(z=(net.z + j) % 16))
+            net.start(("dot_z", j), dot_z.at[0], dot_z.at[j], net.device(z=mod(net.z + j, 16)))
 
     other(0)
     other(1)

time: 124 us -> 124 us (level)
  no operation moved by 1% of the time
where the time goes in v4:
time: 124 us
  Pallas kernels  117 us (94%)
  local copies, waits for them, and re-layouts  5.53 us (4%)
  between operations  1.31 us (1%)
    pallas_call x1, Pallas kernels, local(): pl.pallas_call(kernel, out_shape=jax.ShapeDtypeStruct((16, 384), F32), in...  117 us
    unnamed x4, local copies, waits for them, and re-layouts  5.53 us

profile of v4, /device:TPU:1, one launch (start us, length us, event | category | flops | bytes accessed | tf_op | source)
XLA Modules:
  0.0 124.1 jit_solution(11821000589856754621)
XLA Ops:
  1.3 1.4 %copy.13.routes_ref = s32[24,2]{1,0:T(8,128)} copy(s32[24,2]{0,1:T(2,128)} %param.15) | data formatting | bytes 384 | tf_op args[4]
  2.7 1.4 %copy.14.route_weight_ref = f32[24,2]{1,0:T(8,128)} copy(f32[24,2]{0,1:T(2,128)} %param.16) | data formatting | bytes 384 | tf_op args[5]
  4.0 1.5 %copy.12.ids_ref = s32[256,24]{1,0:T(8,128)} copy(s32[256,24]{0,1:T(8,128)} %param.12) | data formatting | bytes 49152 | tf_op args[1]
  5.5 117.3 %moe_backward.1 = f32[16,384]{1,0:T(8,128)} custom-call(bf16[16,384]{1,0:T(8,128)(2,1)} %pool_ref.1, bf16[24,384]{1,0:T(8,128)(2,1)} %cot_ref.1, s32[256,24]{1,0:T(8,128)} %copy.12.ids_ref, s32[1]{0:T(128)S(6)} %copy.16.tenant_ref, s32[1]{0:T(128)S(6)} %copy.17.lengths_ref, s32[24,2]{1,0:T(8,128)} %copy.13.routes_ref, f32[24,2]{1,0:T(8,128)} %copy.14.route_weight_ref, ...), custom_call_target="tpu_custom_call" | custom-call | tf_op jit(solution)/shard_map/moe_backward/pallas_call | solution.py:759
  122.7 1.3 %copy.18 = f32[16,384]{1,0:T(8,128)} copy(f32[16,384]{1,0:T(8,128)} %moe_backward.1) | data formatting | bytes 49152
